TPU v7x, 512 devices: a whole 4x8x8 slice. The times are simulated.
512 devices in a mesh: fsdp: 32 (over x, z_hi, core), replica: 16 (over y, z_lo).
Axes of the slice: x: 4, y: 8, z: 8 (z_hi: 4, z_lo: 2; z = z_hi * 2 + z_lo), core: 2. Of those that a mesh axis runs over, the one named last changes fastest.
Arguments:
- tokens: bfloat16 [16, 2048, 4096], P('replica', 'fsdp'), may hold values from -6 to 6
- cotangent: bfloat16 [16, 8192, 896], P('replica', 'fsdp'), may hold values from -0.29882812 to 0.29882812
- master: float32 [16, 4096, 896], P('replica', 'fsdp'), may hold values from -0.09375 to 0.09375
- moment_one: float32 [16, 4096, 896], P('replica', 'fsdp'), may hold values from -3 to 3
- moment_two: float32 [16, 4096, 896], P('replica', 'fsdp'), may hold values from 0.5 to 5
- anchor: float32 [4, 4, 32768], P(None, None, 'fsdp'), may hold values from -6 to 6
- outer_momentum: float32 [4, 4, 32768], P(None, None, 'fsdp'), may hold values from -3 to 3
- local_frag: bfloat16 [16, 4, 32768], P('replica', None, 'fsdp'), may hold values from -6 to 6
- frag_index: int32 [1], replicated, may hold values from 0 to 3
Outputs:
- new_master: float32 [16, 4096, 896], P('replica', 'fsdp')
- new_moment_one: float32 [16, 4096, 896], P('replica', 'fsdp')
- new_moment_two: float32 [16, 4096, 896], P('replica', 'fsdp')
- up_values: bfloat16 [16, 8192, 896], P('replica', 'fsdp')
- new_anchor: float32 [4, 32768], P(None, 'fsdp')
- new_momentum: float32 [4, 32768], P(None, 'fsdp')
All inputs are finite; a program needn't handle non-finite values.
Results may differ from a plain program's by a relative error of at most 0.009.
Values may be sent and summed in bfloat16 or wider, within the bound.
A program may use at most 128 MiB of HBM per device.

v0:
```python
import jax
import jax.numpy as jnp
from jax import lax
from jax.sharding import PartitionSpec as P

HGROUP = 4


beta_one = 0.9
beta_two = 0.95
adam_eps = 1e-08
inner_rate = 0.0003
decay_rate = 0.1
correct_one = 1.0 - 0.9**20
correct_two = 1.0 - 0.95**20
outer_rate = 0.7
outer_mu = 0.9


def partner_2(value, axis, distance):
    mask = 2**distance
    pairs = [(source, source ^ mask) for source in range(lax.axis_size(axis))]
    return lax.ppermute(value, axis, pairs)


def adam_update(master, moment_one, moment_two, grad):
    new_one = beta_one * moment_one + (1.0 - beta_one) * grad
    new_two = beta_two * moment_two + (1.0 - beta_two) * grad * grad
    step_dir = new_one / correct_one / (jnp.sqrt(new_two / correct_two) + adam_eps)
    new_master = master - inner_rate * (step_dir + decay_rate * master)
    return (new_master, new_one, new_two)


def nesterov(anchor_part, momentum_part, delta):
    new_momentum = outer_mu * momentum_part + delta
    new_anchor = anchor_part - outer_rate * (outer_mu * new_momentum + delta)
    return (new_anchor, new_momentum)


def local(
    tokens,
    cotangent,
    master,
    moment_one,
    moment_two,
    anchor,
    outer_momentum,
    local_frag,
    frag_index,
):
    position = lax.axis_index("replica")
    group = tokens[0]
    for level in range(HGROUP.bit_length() - 1):
        partner = partner_2(group, "replica", level)
        upper = position // (1 << level) % 2
        group = jnp.where(
            upper == 0, jnp.concatenate([group, partner], 0), jnp.concatenate([partner, group], 0)
        )
    weights = master[0].astype(jnp.bfloat16)
    sums = jnp.dot(
        group,
        lax.all_gather(weights, "fsdp", axis=0, tiled=True),
        preferred_element_type=jnp.float32,
    )
    up_values = sums.astype(jnp.bfloat16)
    upstream = cotangent[0]
    token_cols = lax.all_to_all(group, "fsdp", split_axis=1, concat_axis=0, tiled=True)
    upstream_all = lax.all_gather(upstream, "fsdp", axis=0, tiled=True)
    grad = jnp.einsum("td,th->dh", token_cols, upstream_all, preferred_element_type=jnp.float32)
    new_master, new_one, new_two = adam_update(master[0], moment_one[0], moment_two[0], grad)
    fragment = frag_index[0]
    anchor_frag = lax.dynamic_index_in_dim(anchor, fragment, 0, keepdims=False)
    momentum_frag = lax.dynamic_index_in_dim(outer_momentum, fragment, 0, keepdims=False)
    local_sel = lax.dynamic_index_in_dim(local_frag[0], fragment, 0, keepdims=False).astype(
        jnp.float32
    )
    quarter = position % HGROUP
    own_anchor = lax.dynamic_index_in_dim(anchor_frag, quarter, 0, keepdims=False)
    slot_mask = (jnp.arange(HGROUP, dtype=jnp.int32) == quarter).astype(jnp.float32)
    own_delta = slot_mask[:, None] * (own_anchor - local_sel)[None, :]
    replicas = lax.axis_size("replica") // HGROUP
    delta = lax.psum(own_delta, "replica") / replicas
    new_anchor, new_momentum = nesterov(anchor_frag, momentum_frag, delta)
    return (
        new_master[None],
        new_one[None],
        new_two[None],
        up_values[None],
        new_anchor,
        new_momentum,
    )


def solution(mesh):
    in_specs = (
        P("replica", "fsdp", None),
        P("replica", "fsdp", None),
        P("replica", "fsdp", None),
        P("replica", "fsdp", None),
        P("replica", "fsdp", None),
        P(None, None, "fsdp"),
        P(None, None, "fsdp"),
        P("replica", None, "fsdp"),
        P(),
    )
    out_specs = (
        P("replica", "fsdp", None),
        P("replica", "fsdp", None),
        P("replica", "fsdp", None),
        P("replica", "fsdp", None),
        P(None, "fsdp"),
        P(None, "fsdp"),
    )
    return jax.shard_map(local, mesh=mesh, in_specs=in_specs, out_specs=out_specs, check_vma=False)
```

profile of v0, /device:TPU:1, one launch (start us, length us, event | category | flops | bytes accessed | tf_op | source)
XLA Modules:
  0.0 274.8 jit_solution(6892045307299493167)
XLA Ops:
  7.2 0.0 all-gather.4.cloned.1.call-start
  7.2 1.7 bitcast_convert_fusion
  8.9 0.0 all-gather.4.cloned.1.call-update
  9.0 0.0 all-gather.6.cloned.1.call-start
  9.0 0.7 all-gather.6.cloned.1.call-update
  9.7 4.8 %collective-permute-start = (bf16[64,4096]{1,0:T(8,128)(2,1)}, bf16[64,4096]{1,0:T(8,128)(2,1)S(1)}, u32[]{:S(2)}, u32[]{:S(2)}) collective-permute-start(bf16[64,4096]{1,0:T(8,128)(2,1)} %bitcast.62), channel_id=1, source_target_pairs={{0,1},{1,0},{2,3},{3,2},{4,5},{5,4},{6,7},{7,6},{8,9},{9,8},{10,11... | collective-permute-start | bytes 1572872 | tf_op jit(solution)/shard_map/ppermute | solution.py:23
  14.6 1.5 copy.20
  16.1 0.0 copy-start
  16.1 6.3 %collective-permute-done = bf16[64,4096]{1,0:T(8,128)(2,1)S(1)} collective-permute-done((bf16[64,4096]{1,0:T(8,128)(2,1)}, bf16[64,4096]{1,0:T(8,128)(2,1)S(1)}, u32[]{:S(2)}, u32[]{:S(2)}) %collective-permute-start) | collective-permute-done | bytes 524320 | tf_op jit(solution)/shard_map/ppermute | solution.py:23
  22.4 0.5 copy.22
  22.9 2.2 maximum_select_fusion.8
  25.0 7.2 %collective-permute-start.1 = (bf16[128,4096]{0,1:T(8,128)(2,1)}, bf16[128,4096]{0,1:T(8,128)(2,1)}, u32[]{:S(2)}, u32[]{:S(2)}) collective-permute-start(bf16[128,4096]{0,1:T(8,128)(2,1)} %maximum_select_fusion.8), channel_id=1, source_target_pairs={{0,2},{1,3},{2,0},{3,1},{4,6},{5,7},{6,4},{7,5},{8,10},{9,11},{10,... | collective-permute-start | bytes 3145736 | tf_op jit(solution)/shard_map/ppermute | solution.py:23
  32.3 0.0 copy-done
  32.3 0.1 copy.28
  32.4 0.1 copy.29
  32.5 0.2 maximum_select_fusion.7
  32.7 21.4 %collective-permute-done.1 = bf16[128,4096]{0,1:T(8,128)(2,1)} collective-permute-done((bf16[128,4096]{0,1:T(8,128)(2,1)}, bf16[128,4096]{0,1:T(8,128)(2,1)}, u32[]{:S(2)}, u32[]{:S(2)}) %collective-permute-start.1) | collective-permute-done | bytes 1048608 | tf_op jit(solution)/shard_map/ppermute | solution.py:23
  54.1 1.9 copy.24
  56.0 0.3 maximum_select_fusion
  56.4 2.2 copy.26
  58.6 14.8 %all-to-all-start = ((bf16[256,32,128]{2,0,1:T(8,128)(2,1)}), bf16[256,32,128]{2,0,1:T(8,128)(2,1)S(1)}, u32[]{:S(2)}, u32[]{:S(2)}) async-start(bf16[256,32,128]{2,0,1:T(8,128)(2,1)} %copy.26), calls=%async_computation | async-start | bytes 4194304 | tf_op jit(solution)/shard_map/all_to_all | solution.py:67
  74.1 0.0 copy-done.4
  74.1 0.7 convert_subtract_fusion
  74.8 0.1 broadcast_multiply_fusion
  74.9 108.8 %psum.7 = f32[4,1024]{1,0:T(4,128)S(1)} all-reduce(f32[4,1024]{1,0:T(4,128)S(1)} %broadcast_multiply_fusion), channel_id=1, replica_groups=mesh['fsdp'=32,'replica'=16] {'replica'}, use_global_device_ids=true, to_apply=%region_0.1 | all-reduce | flops 4096 | bytes 32768 | tf_op jit(solution)/shard_map/psum | solution.py:82
  183.7 1.4 bitcast_subtract_fusion.1
  185.1 0.0 all-gather.4.cloned.1.call-done
  185.1 7.6 %fusion.10 = bf16[1,256,896]{2,1,0:T(8,128)(2,1)} fusion(bf16[4096,896]{1,0:T(8,128)(2,1)} %all-gather.4.cloned.1.call-done, bf16[128,4096]{0,1:T(8,128)(2,1)} %collective-permute-done.1, bf16[128,4096]{0,1:T(8,128)(2,1)} %maximum_select_fusion.8, pred[]{:T(512)S(6)} %eq.20), kind=kOutput, calls=%fused_computation.12 | convolution fusion | flops 1888714752 | bytes 9895937 | tf_op jit(solution)/shard_map/dot_general | solution.py:60
  192.7 0.0 all-to-all-done
  192.7 66.4 %all-gather.6.cloned.1.call-done = bf16[1,8192,896]{2,1,0:T(8,128)(2,1)} async-done(((bf16[1,256,896]{2,1,0:T(8,128)(2,1)}), bf16[1,8192,896]{2,1,0:T(8,128)(2,1)}) %all-gather.6.cloned.1.call-update) | async-done | bytes 14680080 | tf_op jit(solution)/shard_map/all_gather | solution.py:68
  259.1 0.0 copy-done.1
  259.1 8.9 %fusion.16 = (f32[1,128,896]{2,1,0:T(8,128)}, f32[1,128,896]{2,1,0:T(8,128)}, f32[1,128,896]{2,1,0:T(8,128)}) fusion(f32[1,128,896]{2,1,0:T(8,128)S(1)} %copy-done.2, f32[1,128,896]{2,1,0:T(8,128)S(1)} %copy-done.3, f32[1,128,896]{2,1,0:T(8,128)S(1)} %copy-done.1, bf16[8192,128]{1,0:T(8,128)(2,1)S(1)} %bitcast.60, ...), kind=kOutput, calls=%fused_computation.25 | convolution fusion | flops 1880768512 | bytes 19529728 | tf_op jit(solution)/shard_map/td,th->dh/dot_general | solution.py:69
  (7 shorter events, 0.0 us)
Async XLA Ops:
  7.2 177.9 %all-gather.4.cloned.1.call-start = ((), (), s32[]{:S(2)}) async-start(), calls=%async_computation.1 | async-start | bytes 7569408 | tf_op jit(solution)/shard_map/all_gather | solution.py:62
  9.0 250.1 %all-gather.6.cloned.1.call-start = ((), (), s32[]{:S(2)}) async-start(), calls=%async_computation.2 | async-start | bytes 15138816 | tf_op jit(solution)/shard_map/all_gather | solution.py:68
  9.7 12.7 %collective-permute-start = (bf16[64,4096]{1,0:T(8,128)(2,1)}, bf16[64,4096]{1,0:T(8,128)(2,1)S(1)}, u32[]{:S(2)}, u32[]{:S(2)}) collective-permute-start(bf16[64,4096]{1,0:T(8,128)(2,1)} %bitcast.62), channel_id=1, source_target_pairs={{0,1},{1,0},{2,3},{3,2},{4,5},{5,4},{6,7},{7,6},{8,9},{9,8},{10,11... | collective-permute-start | bytes 1572872 | tf_op jit(solution)/shard_map/ppermute | solution.py:23
  16.1 16.2 %copy-start = (bf16[1,64,4096]{2,1,0:T(8,128)(2,1)S(1)}, bf16[1,64,4096]{2,1,0:T(8,128)(2,1)}, u32[]{:S(2)}) copy-start(bf16[1,64,4096]{2,1,0:T(8,128)(2,1)} %param.9) | copy-start | bytes 1572868
  25.0 29.1 %collective-permute-start.1 = (bf16[128,4096]{0,1:T(8,128)(2,1)}, bf16[128,4096]{0,1:T(8,128)(2,1)}, u32[]{:S(2)}, u32[]{:S(2)}) collective-permute-start(bf16[128,4096]{0,1:T(8,128)(2,1)} %maximum_select_fusion.8), channel_id=1, source_target_pairs={{0,2},{1,3},{2,0},{3,1},{4,6},{5,7},{6,4},{7,5},{8,10},{9,11},{10,... | collective-permute-start | bytes 3145736 | tf_op jit(solution)/shard_map/ppermute | solution.py:23
  58.6 15.5 %copy-start.4 = (bf16[1,4,1024]{2,1,0:T(4,128)(2,1)S(1)}, bf16[1,4,1024]{2,1,0:T(4,128)(2,1)}, u32[]{:S(2)}) copy-start(bf16[1,4,1024]{2,1,0:T(4,128)(2,1)} %param.16) | copy-start | bytes 24580
  58.6 134.2 %all-to-all-start = ((bf16[256,32,128]{2,0,1:T(8,128)(2,1)}), bf16[256,32,128]{2,0,1:T(8,128)(2,1)S(1)}, u32[]{:S(2)}, u32[]{:S(2)}) async-start(bf16[256,32,128]{2,0,1:T(8,128)(2,1)} %copy.26), calls=%async_computation | async-start | bytes 4194304 | tf_op jit(solution)/shard_map/all_to_all | solution.py:67
  185.1 74.0 %copy-start.1 = (f32[1,128,896]{2,1,0:T(8,128)S(1)}, f32[1,128,896]{2,1,0:T(8,128)}, u32[]{:S(2)}) copy-start(f32[1,128,896]{2,1,0:T(8,128)} %param.11) | copy-start | bytes 1376260
  185.1 74.0 %copy-start.2 = (f32[1,128,896]{2,1,0:T(8,128)S(1)}, f32[1,128,896]{2,1,0:T(8,128)}, u32[]{:S(2)}) copy-start(f32[1,128,896]{2,1,0:T(8,128)} %param.13) | copy-start | bytes 1376260
  185.1 74.0 %copy-start.3 = (f32[1,128,896]{2,1,0:T(8,128)S(1)}, f32[1,128,896]{2,1,0:T(8,128)}, u32[]{:S(2)}) copy-start(f32[1,128,896]{2,1,0:T(8,128)} %param.12) | copy-start | bytes 1376260
Sparse Core Ops, SparseCore 0:
  11.7 127.8 all-gather.3
  142.7 116.3 all-gather.5
where the time goes:
time: 275 us
  blocking collectives  109 us (40%)
  waiting for transfers between devices  94.8 us (34%)
  starting transfers between devices  26.9 us (10%)
  matrix products  16.5 us (6%)
  between operations  14.9 us (5%)
  other arithmetic  6.56 us (2%)
  local copies, waits for them, and re-layouts  6.3 us (2%)
    psum x1, blocking collectives, local(): delta = lax.psum(own_delta, 'replica') / replicas  109 us
    all_gather x1, waiting for transfers between devices, local(): upstream_all = lax.all_gather(upstream, 'fsdp', axis=0, tiled=True)  66.4 us
    ppermute x2, waiting for transfers between devices, partner_2(): return lax.ppermute(value, axis, pairs)  27.7 us
    all_to_all x1, starting transfers between devices, local(): lax.all_to_all(group, 'fsdp', split_axis=1, concat_axis=0, tiled=True)  14.8 us
    ppermute x2, starting transfers between devices, partner_2(): return lax.ppermute(value, axis, pairs)  12.1 us
    dot_general x1, matrix products, local(): jnp.einsum('td,th->dh', token_cols, upstream_all, preferred_element_type=...  8.92 us
    dot_general x1, matrix products, local(): jnp.dot(group, lax.all_gather(weights, 'fsdp', axis=0, tiled=True), prefe...  7.59 us
  transfers between devices with their start and end apart: 5, of which 3 were waited for; matrix products, arithmetic and copies ran while one was open for 7% of the time, Pallas kernels for 0%

commit v1 on v0

v1 whole, which is shorter than its diff:
```python
import jax
import jax.numpy as jnp
from jax import lax
from jax.experimental import pallas as pl
from jax.experimental.pallas import tpu as pltpu
from jax.sharding import PartitionSpec as P

MESH = pl.DeviceIdType.MESH
F32 = jnp.float32
BF16 = jnp.bfloat16

beta_one = 0.9
beta_two = 0.95
adam_eps = 1e-08
inner_rate = 0.0003
decay_rate = 0.1
correct_one = 1.0 - 0.9**20
correct_two = 1.0 - 0.95**20
outer_rate = 0.7
outer_mu = 0.9

NX = 4
NZ = 4
QUARTERS = 4
TOK = 64
WIDE = 4096
COLS = WIDE // NX
HID = 896
ROWS = 128
TBLK = QUARTERS * TOK
N_COPIES = 64


def adam_update(master, moment_one, moment_two, grad):
    new_one = beta_one * moment_one + (1.0 - beta_one) * grad
    new_two = beta_two * moment_two + (1.0 - beta_two) * grad * grad
    step_dir = new_one / correct_one / (jnp.sqrt(new_two / correct_two) + adam_eps)
    new_master = master - inner_rate * (step_dir + decay_rate * master)
    return (new_master, new_one, new_two)


def nesterov(anchor_part, momentum_part, delta):
    new_momentum = outer_mu * momentum_part + delta
    new_anchor = anchor_part - outer_rate * (outer_mu * new_momentum + delta)
    return (new_anchor, new_momentum)


def mult(value, by):
    return pl.multiple_of(value, by)


def exchange(
    frag_ref,
    tok,
    cot,
    master,
    anchor,
    local_frag,
    grad_out,
    up_out,
    delta_out,
    tbuf,
    wbuf,
    cbuf,
    acc,
    upf,
    up_far,
    up_near,
    up_in,
    up_got,
    g_core,
    g_core_in,
    g_far,
    g_near,
    g_in,
    g_got,
    o_sum,
    o_in,
    ssem,
    rsem,
):
    fs = lax.axis_index("fsdp")
    rp = lax.axis_index("replica")
    x, zh, k = fs // 8, lax.rem(fs // 2, 4), lax.rem(fs, 2)
    y, zl = rp // 2, lax.rem(rp, 2)
    yl = lax.rem(y, 2)
    c = lax.rem(rp, 4)
    c_l = 2 * yl + (1 - zl)
    c_y = 2 * (1 - yl) + zl

    def at(dx=0, dz=0, core=k, yy=y, ll=zl):
        return (lax.rem(x + dx, 4) * 8 + lax.rem(zh + dz, 4) * 2 + core, yy * 2 + ll)

    def flip(bit):
        return y + bit * (1 - 2 * lax.rem(y // bit, 2))

    xp, x2, xm = at(1), at(2), at(3)
    zp, zm = at(0, 1), at(0, 3)
    co = at(core=1 - k)
    py, pl_ = at(yy=flip(1)), at(ll=1 - zl)
    y2, y4 = at(yy=flip(2)), at(yy=flip(4))

    barrier = pltpu.get_barrier_semaphore()
    partners = (xp, x2, xm, zp, zm, co, py, pl_, y2, y4)
    for partner in partners:
        pl.semaphore_signal(barrier, inc=1, device_id=partner, device_id_type=MESH)

    started = []

    def send(src, dst, to):
        number = len(started)
        copy = pltpu.make_async_remote_copy(
            src_ref=src,
            dst_ref=dst,
            send_sem=ssem.at[number],
            recv_sem=rsem.at[number],
            device_id=to,
            device_id_type=MESH,
        )
        copy.start()
        started.append(copy)
        return copy

    def trow(slot, quarter):
        return tbuf.at[pl.ds(mult(slot * TBLK + quarter * TOK, TOK), TOK), :]

    def piece(dx):
        return tok.at[0, :, pl.ds(mult(lax.rem(x + dx, 4) * COLS, COLS), COLS)]

    def woff(dz, core):
        return lax.rem(zh + dz, 4) * (2 * ROWS) + core * ROWS

    def whalf(dz, half):
        return wbuf.at[pl.ds(mult(woff(dz, k) + half * (ROWS // 2), ROWS // 2), ROWS // 2), :]

    def wfull(dz):
        return wbuf.at[pl.ds(mult(woff(dz, k), ROWS), ROWS), :]

    def chalf(slot, half):
        return cbuf.at[slot, pl.ds(half * (TBLK // 2), TBLK // 2), :]

    def own_chalf(half):
        return cot.at[0, pl.ds(half * (TBLK // 2), TBLK // 2), :]

    wbuf[pl.ds(mult(woff(0, k), ROWS), ROWS), :] = master[0].astype(BF16)
    tbuf[pl.ds(mult(c * TOK, TOK), TOK), :] = tok[0, :, pl.ds(mult(x * COLS, COLS), COLS)]

    frag = frag_ref[0]
    anchor_f = anchor[0]
    local_f = local_frag[0, 0:1, :].astype(F32)
    for i in range(1, 4):
        anchor_f = jnp.where(frag == i, anchor[i], anchor_f)
        local_f = jnp.where(frag == i, local_frag[0, i : i + 1, :].astype(F32), local_f)
    quarter = lax.broadcasted_iota(jnp.int32, anchor_f.shape, 0)
    o_sum[0] = jnp.where(quarter == c, anchor_f - local_f, 0.0)

    pl.semaphore_wait(barrier, len(partners))

    t_y = {}
    t_l = {}
    t_r = {}
    t_y[0] = send(trow(0, c), trow(0, c), py)
    t_l[0] = send(trow(0, c), trow(0, c), pl_)
    t_x2 = send(piece(2), trow(2, c), x2)
    t_xp = send(piece(1), trow(3, c), xp)
    t_xm = send(piece(3), trow(1, c), xm)
    w_pa = send(whalf(0, 0), whalf(0, 0), zp)
    w_mb = send(whalf(0, 1), whalf(0, 1), zm)
    c_pa = send(own_chalf(0), chalf(3, 0), xp)
    c_mb = send(own_chalf(1), chalf(1, 1), xm)
    w_pb = send(whalf(0, 1), whalf(0, 1), zp)
    w_ma = send(whalf(0, 0), whalf(0, 0), zm)
    c_pb = send(own_chalf(1), chalf(3, 1), xp)
    c_ma = send(own_chalf(0), chalf(1, 0), xm)
    w_co = [send(wfull(0), wfull(0), co)]
    o_copy = send(o_sum.at[0], o_in.at[0], y2)

    def outer_step(step, copy, to):
        copy.wait_recv()
        o_sum[step] = o_sum[step - 1] + o_in[step - 1]
        if to is None:
            return None
        return send(o_sum.at[step], o_in.at[step], to)

    for slot, copy in ((2, t_x2), (3, t_xp), (1, t_xm)):
        copy.wait_recv()
        t_l[slot] = send(trow(slot, c), trow(slot, c), pl_)
        t_y[slot] = send(trow(slot, c), trow(slot, c), py)

    t_l[0].wait_recv()
    t_r[0] = send(trow(0, c_l), trow(0, c_l), py)
    o_copy = outer_step(1, o_copy, y4)

    w_pa.wait_recv()
    w_ra = send(whalf(3, 0), whalf(3, 0), zp)
    w_mb.wait_recv()
    w_rb = send(whalf(1, 1), whalf(1, 1), zm)
    c_pa.wait_recv()
    c_ra = send(chalf(3, 0), chalf(2, 0), xp)
    c_mb.wait_recv()
    c_rb = send(chalf(1, 1), chalf(2, 1), xm)
    for slot in (2, 3, 1):
        t_l[slot].wait_recv()
        t_r[slot] = send(trow(slot, c_l), trow(slot, c_l), py)
    o_copy = outer_step(2, o_copy, pl_)
    w_pb.wait_recv()
    w_co.append(send(wfull(3), wfull(3), co))
    w_ma.wait_recv()
    w_co.append(send(wfull(1), wfull(1), co))
    o_copy = outer_step(3, o_copy, py)

    def add_grad(slot, first=False):
        part = cot.at[0] if slot == 0 else cbuf.at[slot]

        def tile(j, carry):
            cols = pl.ds(mult(j * 256, 256), 256)
            left = tbuf[slot * TBLK : (slot + 1) * TBLK, cols]
            prod = lax.dot_general(left, part[...], (((0,), (0,)), ((), ())), preferred_element_type=F32)
            if first:
                acc[cols, :] = prod
            else:
                acc[cols, :] += prod
            return carry

        lax.fori_loop(0, COLS // 256, tile, 0)

    def up_part(slot, store):
        left = slice(slot * TBLK, (slot + 1) * TBLK)
        for lo in range(0, HID, 256):
            hi = min(lo + 256, HID)
            store(lo, hi, jnp.dot(tbuf[left, :], wbuf[:, lo:hi], preferred_element_type=F32))

    def tokens_here(slot):
        t_y[slot].wait_recv()
        t_r[slot].wait_recv()

    tokens_here(0)
    add_grad(0, True)

    w_ra.wait_recv()
    w_co.append(send(whalf(2, 0), whalf(2, 0), co))
    w_rb.wait_recv()
    w_co.append(send(whalf(2, 1), whalf(2, 1), co))
    outer_step(4, o_copy, None)

    c_ra.wait_recv()
    c_rb.wait_recv()
    c_pb.wait_recv()
    c_ma.wait_recv()
    tokens_here(2)
    add_grad(2)
    for copy in w_co:
        copy.wait_recv()

    half_t = TBLK // 2
    half_r = ROWS // 2

    def store_far(lo, hi, value):
        up_far[:, lo:hi] = value.astype(BF16)

    def store_f(i):
        def store(lo, hi, value):
            upf[i, :, lo:hi] = value

        return store

    up_part(2, store_far)
    u_fp = send(up_far.at[pl.ds(0, half_t), :], up_in.at[0], xp)
    u_fm = send(up_far.at[pl.ds(half_t, half_t), :], up_in.at[1], xm)

    tokens_here(3)
    add_grad(3)
    tokens_here(1)
    add_grad(1)

    for e in (2, 1, 3, 0):
        rows = pl.ds(mult(woff(e, 1 - k), ROWS), ROWS)
        g_core[e] = acc[rows, :].astype(BF16)
        started_core = send(g_core.at[e], g_core_in.at[e], co)
        if e == 2:
            core_copies = {}
        core_copies[e] = started_core

    up_part(1, store_f(1))
    up_near[0, half_t:, :] = upf[1, half_t:, :].astype(BF16)
    u_pb = send(up_near.at[0, pl.ds(half_t, half_t), :], up_got.at[0, pl.ds(half_t, half_t), :], xp)
    up_part(3, store_f(2))
    up_near[1, :half_t, :] = upf[2, :half_t, :].astype(BF16)
    u_ma = send(up_near.at[1, pl.ds(0, half_t), :], up_got.at[1, pl.ds(0, half_t), :], xm)

    def core_sum(e):
        rows = pl.ds(mult(woff(e, k), ROWS), ROWS)
        core_copies[e].wait_recv()
        total = acc[rows, :] + g_core_in[e].astype(F32)
        acc[rows, :] = total
        return total

    g_far[...] = core_sum(2).astype(BF16)
    g_fp = send(g_far.at[pl.ds(0, half_r), :], g_in.at[0], zp)
    g_fm = send(g_far.at[pl.ds(half_r, half_r), :], g_in.at[1], zm)
    g_near[0] = core_sum(1).astype(BF16)
    g_pb = send(g_near.at[0, pl.ds(half_r, half_r), :], g_got.at[0, pl.ds(half_r, half_r), :], zp)
    g_near[1] = core_sum(3).astype(BF16)
    g_ma = send(g_near.at[1, pl.ds(0, half_r), :], g_got.at[1, pl.ds(0, half_r), :], zm)
    core_sum(0)
    up_part(0, store_f(0))

    u_fp.wait_recv()
    up_near[0, :half_t, :] = (upf[1, :half_t, :] + up_in[0].astype(F32)).astype(BF16)
    u_pa = send(up_near.at[0, pl.ds(0, half_t), :], up_got.at[0, pl.ds(0, half_t), :], xp)
    u_fm.wait_recv()
    up_near[1, half_t:, :] = (upf[2, half_t:, :] + up_in[1].astype(F32)).astype(BF16)
    u_mb = send(up_near.at[1, pl.ds(half_t, half_t), :], up_got.at[1, pl.ds(half_t, half_t), :], xm)

    def row_half(dz, half):
        return pl.ds(mult(woff(dz, k) + half * half_r, half_r), half_r)

    g_fp.wait_recv()
    g_near[0, :half_r, :] = (acc[row_half(1, 0), :] + g_in[0].astype(F32)).astype(BF16)
    g_pa = send(g_near.at[0, pl.ds(0, half_r), :], g_got.at[0, pl.ds(0, half_r), :], zp)
    g_fm.wait_recv()
    g_near[1, half_r:, :] = (acc[row_half(3, 1), :] + g_in[1].astype(F32)).astype(BF16)
    g_mb = send(g_near.at[1, pl.ds(half_r, half_r), :], g_got.at[1, pl.ds(half_r, half_r), :], zm)

    delta_out[...] = o_sum[4] * 0.25

    u_pb.wait_recv()
    u_ma.wait_recv()
    u_pa.wait_recv()
    u_mb.wait_recv()
    up_out[0] = (upf[0] + up_got[0].astype(F32) + up_got[1].astype(F32)).astype(BF16)
    g_pb.wait_recv()
    g_ma.wait_recv()
    g_pa.wait_recv()
    g_mb.wait_recv()
    own = pl.ds(mult(woff(0, k), ROWS), ROWS)
    grad_out[...] = acc[own, :] + g_got[0].astype(F32) + g_got[1].astype(F32)

    for copy in started:
        copy.wait_send()


def run_exchange(frag_index, tokens, cotangent, master, anchor, local_frag):
    vmem = pl.BlockSpec(memory_space=pltpu.VMEM)
    return pl.pallas_call(
        exchange,
        name="exchange",
        out_shape=(
            jax.ShapeDtypeStruct((ROWS, HID), F32),
            jax.ShapeDtypeStruct((1, TBLK, HID), BF16),
            jax.ShapeDtypeStruct((QUARTERS, 1024), F32),
        ),
        in_specs=[pl.BlockSpec(memory_space=pltpu.SMEM)] + [vmem] * 5,
        out_specs=(vmem, vmem, vmem),
        scratch_shapes=[
            pltpu.VMEM((NX * TBLK, COLS), BF16),
            pltpu.VMEM((COLS, HID), BF16),
            pltpu.VMEM((NX, TBLK, HID), BF16),
            pltpu.VMEM((COLS, HID), F32),
            pltpu.VMEM((3, TBLK, HID), F32),
            pltpu.VMEM((TBLK, HID), BF16),
            pltpu.VMEM((2, TBLK, HID), BF16),
            pltpu.VMEM((2, TBLK // 2, HID), BF16),
            pltpu.VMEM((2, TBLK, HID), BF16),
            pltpu.VMEM((4, ROWS, HID), BF16),
            pltpu.VMEM((4, ROWS, HID), BF16),
            pltpu.VMEM((ROWS, HID), BF16),
            pltpu.VMEM((2, ROWS, HID), BF16),
            pltpu.VMEM((2, ROWS // 2, HID), BF16),
            pltpu.VMEM((2, ROWS, HID), BF16),
            pltpu.VMEM((5, QUARTERS, 1024), F32),
            pltpu.VMEM((4, QUARTERS, 1024), F32),
            pltpu.SemaphoreType.DMA((N_COPIES,)),
            pltpu.SemaphoreType.DMA((N_COPIES,)),
        ],
        compiler_params=pltpu.CompilerParams(
            collective_id=0, has_side_effects=True, vmem_limit_bytes=48 * 2**20
        ),
    )(frag_index, tokens, cotangent, master, anchor, local_frag)


def local(
    tokens,
    cotangent,
    master,
    moment_one,
    moment_two,
    anchor,
    outer_momentum,
    local_frag,
    frag_index,
):
    grad, up_values, delta = run_exchange(frag_index, tokens, cotangent, master, anchor, local_frag)
    new_master, new_one, new_two = adam_update(master[0], moment_one[0], moment_two[0], grad)
    fragment = frag_index[0]
    anchor_frag = lax.dynamic_index_in_dim(anchor, fragment, 0, keepdims=False)
    momentum_frag = lax.dynamic_index_in_dim(outer_momentum, fragment, 0, keepdims=False)
    new_anchor, new_momentum = nesterov(anchor_frag, momentum_frag, delta)
    return (
        new_master[None],
        new_one[None],
        new_two[None],
        up_values,
        new_anchor,
        new_momentum,
    )


def solution(mesh):
    in_specs = (
        P("replica", "fsdp", None),
        P("replica", "fsdp", None),
        P("replica", "fsdp", None),
        P("replica", "fsdp", None),
        P("replica", "fsdp", None),
        P(None, None, "fsdp"),
        P(None, None, "fsdp"),
        P("replica", None, "fsdp"),
        P(),
    )
    out_specs = (
        P("replica", "fsdp", None),
        P("replica", "fsdp", None),
        P("replica", "fsdp", None),
        P("replica", "fsdp", None),
        P(None, "fsdp"),
        P(None, "fsdp"),
    )
    return jax.shard_map(local, mesh=mesh, in_specs=in_specs, out_specs=out_specs, check_vma=False)
```

time: 275 us -> 77.7 us (0.28)
  the two profiles are of different devices: /device:TPU:1 before, /device:TPU:66 now
where the time goes in v1:
time: 77.7 us; the launch traced here: 77.3 us
  Pallas kernels  67.8 us (87%)
  local copies, waits for them, and re-layouts  5.38 us (7%)
  other arithmetic  2.78 us (4%)
  between operations  1.32 us (2%)
    pallas_call x1, Pallas kernels, run_exchange(): pl.pallas_call(exchange, name='exchange', out_shape=(jax.ShapeDtypeStruct...  67.8 us
    unnamed x15, local copies, waits for them, and re-layouts  5.38 us

profile of v1, /device:TPU:66, one launch (start us, length us, event | category | flops | bytes accessed | tf_op | source)
XLA Modules:
  0.0 77.3 jit_solution(8873794786720920712)
XLA Ops:
  1.3 0.0 copy-start
  1.3 1.0 %copy-done = f32[1,128,896]{2,1,0:T(8,128)S(1)} copy-done((f32[1,128,896]{2,1,0:T(8,128)S(1)}, f32[1,128,896]{2,1,0:T(8,128)}, u32[]{:S(2)}) %copy-start) | copy-done | bytes 458776
  2.3 0.0 copy-start.1
  2.3 1.0 %copy-done.1 = bf16[1,64,4096]{2,1,0:T(8,128)(2,1)S(1)} copy-done((bf16[1,64,4096]{2,1,0:T(8,128)(2,1)S(1)}, bf16[1,64,4096]{2,1,0:T(8,128)(2,1)}, u32[]{:S(2)}) %copy-start.1) | copy-done | bytes 524312
  3.3 0.0 copy-start.2
  3.3 1.0 %copy-done.2 = bf16[1,256,896]{2,1,0:T(8,128)(2,1)S(1)} copy-done((bf16[1,256,896]{2,1,0:T(8,128)(2,1)S(1)}, bf16[1,256,896]{2,1,0:T(8,128)(2,1)}, u32[]{:S(2)}) %copy-start.2) | copy-done | bytes 458776
  4.4 0.0 copy-start.3
  4.4 0.8 %copy-done.3 = f32[4,4,1024]{2,1,0:T(4,128)S(1)} copy-done((f32[4,4,1024]{2,1,0:T(4,128)S(1)}, f32[4,4,1024]{2,1,0:T(4,128)}, u32[]{:S(2)}) %copy-start.3) | copy-done | bytes 65560
  5.2 0.0 copy-start.4
  5.2 0.7 copy-done.4
  5.9 0.0 copy-start.5
  5.9 0.0 copy-start.6
  5.9 67.8 %exchange.1 = (f32[128,896]{1,0:T(8,128)S(1)}, bf16[1,256,896]{2,1,0:T(8,128)(2,1)S(1)}, f32[4,1024]{1,0:T(4,128)S(1)}) custom-call(s32[1]{0:T(128)} %copy.16.frag_ref, bf16[1,64,4096]{2,1,0:T(8,128)(2,1)S(1)} %copy-done.1, bf16[1,256,896]{2,1,0:T(8,128)(2,1)S(1)} %copy-done.2, f32[1,128,896]{2,1,0:T(8,128)S(1)} %copy-done, f32[4,4,1024]{2,1,0:T(4,128)S(1)} %copy-done.3, ...), custom_call_target="tpu_custom_call" | custom-call | tf_op jit(solution)/shard_map/exchange/pallas_call | solution.py:345
  73.7 0.0 copy-done.5
  73.8 0.0 copy-done.6
  73.8 1.4 %fusion.5 = (f32[1,128,896]{2,1,0:T(8,128)}, f32[1,128,896]{2,1,0:T(8,128)}, f32[1,128,896]{2,1,0:T(8,128)}) fusion(f32[128,896]{1,0:T(8,128)S(1)} %get-tuple-element.9, f32[1,128,896]{2,1,0:T(8,128)S(1)} %copy-done.5, f32[1,128,896]{2,1,0:T(8,128)S(1)} %copy-done.6, f32[1,128,896]{2,1,0:T(8,128)S(1)} %copy-done), kind=kLoop, calls=%fused_computation.9 | loop fusion | flops 1720320 | bytes 3211264 | tf_op jit(solution)/shard_map/broadcast_in_dim | solution.py:402
  75.2 1.4 %bitcast_subtract_fusion.1 = (f32[4,1024]{1,0:T(4,128)}, f32[4,1024]{1,0:T(4,128)}) fusion(f32[4,1024]{1,0:T(4,128)S(1)} %get-tuple-element.11, f32[4,4,1024]{2,1,0:T(4,128)} %anchor.1, s32[]{:T(128)S(6)} %select_n.5, f32[4,4,1024]{2,1,0:T(4,128)} %param.15), kind=kLoop, calls=%fused_computation.11 | loop fusion | flops 24576 | bytes 81924 | tf_op jit(solution)/shard_map/sub | solution.py:44
  76.5 0.8 copy.17
Async XLA Ops:
  1.3 1.0 %copy-start = (f32[1,128,896]{2,1,0:T(8,128)S(1)}, f32[1,128,896]{2,1,0:T(8,128)}, u32[]{:S(2)}) copy-start(f32[1,128,896]{2,1,0:T(8,128)} %master.1) | copy-start | bytes 1376260
  2.3 1.0 %copy-start.1 = (bf16[1,64,4096]{2,1,0:T(8,128)(2,1)S(1)}, bf16[1,64,4096]{2,1,0:T(8,128)(2,1)}, u32[]{:S(2)}) copy-start(bf16[1,64,4096]{2,1,0:T(8,128)(2,1)} %tok.1) | copy-start | bytes 1572868
  3.3 1.0 %copy-start.2 = (bf16[1,256,896]{2,1,0:T(8,128)(2,1)S(1)}, bf16[1,256,896]{2,1,0:T(8,128)(2,1)}, u32[]{:S(2)}) copy-start(bf16[1,256,896]{2,1,0:T(8,128)(2,1)} %cot.1) | copy-start | bytes 1376260
  4.4 0.8 %copy-start.3 = (f32[4,4,1024]{2,1,0:T(4,128)S(1)}, f32[4,4,1024]{2,1,0:T(4,128)}, u32[]{:S(2)}) copy-start(f32[4,4,1024]{2,1,0:T(4,128)} %anchor.1) | copy-start | bytes 196612
  5.2 0.7 copy-start.4
  5.9 67.8 %copy-start.5 = (f32[1,128,896]{2,1,0:T(8,128)S(1)}, f32[1,128,896]{2,1,0:T(8,128)}, u32[]{:S(2)}) copy-start(f32[1,128,896]{2,1,0:T(8,128)} %param.13) | copy-start | bytes 1376260
  5.9 67.9 %copy-start.6 = (f32[1,128,896]{2,1,0:T(8,128)S(1)}, f32[1,128,896]{2,1,0:T(8,128)}, u32[]{:S(2)}) copy-start(f32[1,128,896]{2,1,0:T(8,128)} %param.12) | copy-start | bytes 1376260

commit v2 on v1

v2 whole, which is shorter than its diff:
```python
import jax
import jax.numpy as jnp
from jax import lax
from jax.experimental import pallas as pl
from jax.experimental.pallas import tpu as pltpu
from jax.sharding import PartitionSpec as P

MESH = pl.DeviceIdType.MESH
F32 = jnp.float32
BF16 = jnp.bfloat16

beta_one = 0.9
beta_two = 0.95
adam_eps = 1e-08
inner_rate = 0.0003
decay_rate = 0.1
correct_one = 1.0 - 0.9**20
correct_two = 1.0 - 0.95**20
outer_rate = 0.7
outer_mu = 0.9

NX = 4
NZ = 4
QUARTERS = 4
FRAGS = 4
TOK = 64
WIDE = 4096
COLS = WIDE // NX
HID = 896
ROWS = 128
TBLK = QUARTERS * TOK
N_COPIES = 64


def adam_decayed(master, moment_one, moment_two):
    return (master * (1.0 - inner_rate * decay_rate), beta_one * moment_one, beta_two * moment_two)


def adam_update(master, moment_one, moment_two, grad):
    new_one = moment_one + (1.0 - beta_one) * grad
    new_two = moment_two + (1.0 - beta_two) * (grad * grad)
    scale = jnp.sqrt(new_two * (1.0 / correct_two)) + adam_eps
    new_master = master - (inner_rate / correct_one) * (new_one / scale)
    return (new_master, new_one, new_two)


def nesterov(anchor_part, momentum_part, delta):
    new_momentum = outer_mu * momentum_part + delta
    new_anchor = anchor_part - outer_rate * (outer_mu * new_momentum + delta)
    return (new_anchor, new_momentum)


def mult(value, by):
    return pl.multiple_of(value, by)


class Sent:
    def __init__(self, copy):
        self.copy = copy
        self.here = False

    def wait_recv(self):
        if not self.here:
            self.here = True
            self.copy.wait_recv()


def exchange(
    tok,
    cot,
    master,
    local_hbm,
    one_hbm,
    two_hbm,
    master_out,
    one_out,
    two_out,
    up_out,
    sum_out,
    tbuf,
    wbuf,
    cbuf,
    acc,
    upf,
    up_far,
    up_near,
    up_in,
    up_got,
    g_core,
    g_core_in,
    g_far,
    g_near,
    g_in,
    g_got,
    o_part,
    o_in,
    o_all,
    master_v,
    one_v,
    two_v,
    local_frag,
    ssem,
    rsem,
    lsem,
):
    fs = lax.axis_index("fsdp")
    rp = lax.axis_index("replica")
    x, zh, k = fs // 8, lax.rem(fs // 2, 4), lax.rem(fs, 2)
    y, zl = rp // 2, lax.rem(rp, 2)
    yl = lax.rem(y, 2)
    c = lax.rem(rp, 4)
    c_l = 2 * yl + (1 - zl)

    def at(dx=0, dz=0, core=k, yy=y, ll=zl):
        return (lax.rem(x + dx, 4) * 8 + lax.rem(zh + dz, 4) * 2 + core, yy * 2 + ll)

    def flip(bit):
        return y + bit * (1 - 2 * lax.rem(y // bit, 2))

    xp, x2, xm = at(1), at(2), at(3)
    zp, zm = at(0, 1), at(0, 3)
    co = at(core=1 - k)
    py, pl_ = at(yy=flip(1)), at(ll=1 - zl)
    y2, y4 = at(yy=flip(2)), at(yy=flip(4))

    barrier = pltpu.get_barrier_semaphore()
    partners = (xp, x2, xm, zp, zm, co, py, pl_, y2, y4)
    for partner in partners:
        pl.semaphore_signal(barrier, inc=1, device_id=partner, device_id_type=MESH)

    started = []

    def send(src, dst, to):
        number = len(started)
        copy = pltpu.make_async_remote_copy(
            src_ref=src,
            dst_ref=dst,
            send_sem=ssem.at[number],
            recv_sem=rsem.at[number],
            device_id=to,
            device_id_type=MESH,
        )
        copy.start()
        started.append(Sent(copy))
        return started[-1]

    def trow(slot, quarter):
        return tbuf.at[pl.ds(mult(slot * TBLK + quarter * TOK, TOK), TOK), :]

    def piece(dx):
        return tok.at[0, :, pl.ds(mult(lax.rem(x + dx, 4) * COLS, COLS), COLS)]

    def woff(dz, core):
        return lax.rem(zh + dz, 4) * (2 * ROWS) + core * ROWS

    def whalf(dz, half):
        return wbuf.at[pl.ds(mult(woff(dz, k) + half * (ROWS // 2), ROWS // 2), ROWS // 2), :]

    def wfull(dz):
        return wbuf.at[pl.ds(mult(woff(dz, k), ROWS), ROWS), :]

    def chalf(slot, half):
        return cbuf.at[slot, pl.ds(half * (TBLK // 2), TBLK // 2), :]

    def own_chalf(half):
        return cot.at[0, pl.ds(half * (TBLK // 2), TBLK // 2), :]

    loads = [
        pltpu.make_async_copy(src, dst, lsem.at[i])
        for i, (src, dst) in enumerate(
            (
                (master.at[0], master_v),
                (piece(0), trow(0, c)),
                (local_hbm, local_frag),
                (cot.at[0], cbuf.at[0]),
                (one_hbm.at[0], one_v),
                (two_hbm.at[0], two_v),
            )
        )
    ]
    for load in loads:
        load.start()
    l_master, l_tok, l_local, l_cot, l_one, l_two = loads

    l_master.wait()
    wbuf[pl.ds(mult(woff(0, k), ROWS), ROWS), :] = master_v[...].astype(BF16)

    pl.semaphore_wait(barrier, len(partners))

    t_y, t_l, t_r = {}, {}, {}

    cp = {}

    def own_outer():
        for load in (l_tok, l_local, l_cot, l_one, l_two):
            load.wait()
        o_part[0] = local_frag[0].astype(F32)
        cp["o1"] = send(o_part.at[0], o_in.at[0], y2)

    def outer_two():
        cp["o1"].wait_recv()
        o_part[1] = o_part[0] + o_in[0]
        cp["o2"] = send(o_part.at[1], o_in.at[1], y4)

    def outer_three():
        cp["o2"].wait_recv()
        o_all[c] = o_part[1] + o_in[1]
        cp["o3"] = send(o_all.at[c], o_all.at[c], pl_)

    def outer_four():
        cp["o3"].wait_recv()
        o_two = pl.ds(2 * yl, 2)
        cp["o4"] = send(o_all.at[o_two], o_all.at[o_two], py)

    def put(name, src, dst, to):
        def step():
            cp[name] = send(src, dst, to)

        return step

    def after(name, *steps):
        def step():
            cp[name].wait_recv()
            for each in steps:
                each()

        return step

    def t_on(slot):
        def step():
            t_l[slot] = send(trow(slot, c), trow(slot, c), pl_)
            t_y[slot] = send(trow(slot, c), trow(slot, c), py)

        return step

    def t_relay(slot):
        def step():
            t_l[slot].wait_recv()
            t_r[slot] = send(trow(slot, c_l), trow(slot, c_l), py)

        return step

    def t_own():
        t_y[0] = send(piece(0), trow(0, c), py)
        t_l[0] = send(piece(0), trow(0, c), pl_)

    steps = {
        "t_own": t_own,
        "t_xp": put("t_xp", piece(1), trow(3, c), xp),
        "t_xm": put("t_xm", piece(3), trow(1, c), xm),
        "t_x2": put("t_x2", piece(2), trow(2, c), x2),
        "t_on3": after("t_xp", t_on(3)),
        "t_on1": after("t_xm", t_on(1)),
        "t_on2": after("t_x2", t_on(2)),
        "t_re0": t_relay(0),
        "t_re1": t_relay(1),
        "t_re2": t_relay(2),
        "t_re3": t_relay(3),
        "w_pa": put("w_pa", whalf(0, 0), whalf(0, 0), zp),
        "w_mb": put("w_mb", whalf(0, 1), whalf(0, 1), zm),
        "w_pb": put("w_pb", whalf(0, 1), whalf(0, 1), zp),
        "w_ma": put("w_ma", whalf(0, 0), whalf(0, 0), zm),
        "w_ra": after("w_pa", put("w_ra", whalf(3, 0), whalf(3, 0), zp)),
        "w_rb": after("w_mb", put("w_rb", whalf(1, 1), whalf(1, 1), zm)),
        "w_c0": put("w_c0", wfull(0), wfull(0), co),
        "w_c3": after("w_pb", put("w_c3", wfull(3), wfull(3), co)),
        "w_c1": after("w_ma", put("w_c1", wfull(1), wfull(1), co)),
        "w_c2a": after("w_ra", put("w_c2a", whalf(2, 0), whalf(2, 0), co)),
        "w_c2b": after("w_rb", put("w_c2b", whalf(2, 1), whalf(2, 1), co)),
        "c_pa": put("c_pa", own_chalf(0), chalf(3, 0), xp),
        "c_mb": put("c_mb", own_chalf(1), chalf(1, 1), xm),
        "c_pb": put("c_pb", own_chalf(1), chalf(3, 1), xp),
        "c_ma": put("c_ma", own_chalf(0), chalf(1, 0), xm),
        "c_ra": after("c_pa", put("c_ra", chalf(3, 0), chalf(2, 0), xp)),
        "c_rb": after("c_mb", put("c_rb", chalf(1, 1), chalf(2, 1), xm)),
        "o1": own_outer,
        "o2": outer_two,
        "o3": outer_three,
        "o4": outer_four,
    }
    order = (
        "t_own t_xp t_xm t_x2 w_pa w_mb w_c0 o1 t_on3 t_on1 c_pa c_mb t_re0 t_on2 c_pb c_ma w_pb w_ma o2 "
        "w_ra w_rb t_re3 c_ra c_rb t_re1 t_re2 o3 w_c3 w_c1 o4"
    )
    for step in order.split():
        steps[step]()

    def add_grad(slot, first=False):
        part = cbuf.at[slot]

        def tile(j, carry):
            cols = pl.ds(mult(j * 256, 256), 256)
            left = tbuf[slot * TBLK : (slot + 1) * TBLK, cols]
            prod = lax.dot_general(left, part[...], (((0,), (0,)), ((), ())), preferred_element_type=F32)
            if first:
                acc[cols, :] = prod
            else:
                acc[cols, :] += prod
            return carry

        lax.fori_loop(0, COLS // 256, tile, 0)

    def up_part(slot, store):
        left = slice(slot * TBLK, (slot + 1) * TBLK)
        for lo in range(0, HID, 256):
            hi = min(lo + 256, HID)
            store(lo, hi, jnp.dot(tbuf[left, :], wbuf[:, lo:hi], preferred_element_type=F32))

    def tokens_here(slot):
        t_y[slot].wait_recv()
        t_r[slot].wait_recv()

    half_t = TBLK // 2
    half_r = ROWS // 2
    tokens_here(0)
    add_grad(0, True)

    steps["w_c2a"]()
    steps["w_c2b"]()
    cp["o4"].wait_recv()
    sum_out[...] = o_all[...]
    master_v[...], one_v[...], two_v[...] = adam_decayed(master_v[...], one_v[...], two_v[...])

    for name in ("c_ra", "c_rb", "c_pb", "c_ma"):
        cp[name].wait_recv()
    tokens_here(2)
    add_grad(2)
    for name in ("w_c0", "w_c1", "w_c3", "w_c2a", "w_c2b"):
        cp[name].wait_recv()

    def store_far(lo, hi, value):
        up_far[:, lo:hi] = value.astype(BF16)

    def store_f(i):
        def store(lo, hi, value):
            upf[i, :, lo:hi] = value

        return store

    up_part(2, store_far)
    u_fp = send(up_far.at[pl.ds(0, half_t), :], up_in.at[0], xp)
    u_fm = send(up_far.at[pl.ds(half_t, half_t), :], up_in.at[1], xm)

    tokens_here(3)
    add_grad(3)
    up_part(3, store_f(2))
    up_near[1, :half_t, :] = upf[2, :half_t, :].astype(BF16)
    u_ma = send(up_near.at[1, pl.ds(0, half_t), :], up_got.at[1, pl.ds(0, half_t), :], xm)

    tokens_here(1)
    core_copies = {}
    for e in (2, 1, 3, 0):
        both = pl.ds(mult(woff(e, 0), 2 * ROWS), 2 * ROWS)
        left = tbuf[TBLK : 2 * TBLK, both]
        acc[both, :] += lax.dot_general(left, cbuf[1], (((0,), (0,)), ((), ())), preferred_element_type=F32)
        g_core[e] = acc[pl.ds(mult(woff(e, 1 - k), ROWS), ROWS), :].astype(BF16)
        core_copies[e] = send(g_core.at[e], g_core_in.at[e], co)

    def core_sum(e):
        rows = pl.ds(mult(woff(e, k), ROWS), ROWS)
        core_copies[e].wait_recv()
        total = acc[rows, :] + g_core_in[e].astype(F32)
        acc[rows, :] = total
        return total

    g_far[...] = core_sum(2).astype(BF16)
    g_fp = send(g_far.at[pl.ds(0, half_r), :], g_in.at[0], zp)
    g_fm = send(g_far.at[pl.ds(half_r, half_r), :], g_in.at[1], zm)
    g_near[0] = core_sum(1).astype(BF16)
    g_pb = send(g_near.at[0, pl.ds(half_r, half_r), :], g_got.at[0, pl.ds(half_r, half_r), :], zp)
    g_near[1] = core_sum(3).astype(BF16)
    g_ma = send(g_near.at[1, pl.ds(0, half_r), :], g_got.at[1, pl.ds(0, half_r), :], zm)
    core_sum(0)

    up_part(1, store_f(1))
    up_near[0, half_t:, :] = upf[1, half_t:, :].astype(BF16)
    u_pb = send(up_near.at[0, pl.ds(half_t, half_t), :], up_got.at[0, pl.ds(half_t, half_t), :], xp)

    u_fm.wait_recv()
    up_near[1, half_t:, :] = (upf[2, half_t:, :] + up_in[1].astype(F32)).astype(BF16)
    u_mb = send(up_near.at[1, pl.ds(half_t, half_t), :], up_got.at[1, pl.ds(half_t, half_t), :], xm)
    u_fp.wait_recv()
    up_near[0, :half_t, :] = (upf[1, :half_t, :] + up_in[0].astype(F32)).astype(BF16)
    u_pa = send(up_near.at[0, pl.ds(0, half_t), :], up_got.at[0, pl.ds(0, half_t), :], xp)
    up_part(0, store_f(0))

    def row_half(dz, half):
        return pl.ds(mult(woff(dz, k) + half * half_r, half_r), half_r)

    g_fp.wait_recv()
    g_near[0, :half_r, :] = (acc[row_half(1, 0), :] + g_in[0].astype(F32)).astype(BF16)
    g_pa = send(g_near.at[0, pl.ds(0, half_r), :], g_got.at[0, pl.ds(0, half_r), :], zp)
    g_fm.wait_recv()
    g_near[1, half_r:, :] = (acc[row_half(3, 1), :] + g_in[1].astype(F32)).astype(BF16)
    g_mb = send(g_near.at[1, pl.ds(half_r, half_r), :], g_got.at[1, pl.ds(half_r, half_r), :], zm)

    for copy in (u_pb, u_ma, u_pa, u_mb):
        copy.wait_recv()
    up_out[0] = (upf[0] + up_got[0].astype(F32) + up_got[1].astype(F32)).astype(BF16)
    for copy in (g_pb, g_ma, g_pa, g_mb):
        copy.wait_recv()
    own = pl.ds(mult(woff(0, k), ROWS), ROWS)
    grad = acc[own, :] + g_got[0].astype(F32) + g_got[1].astype(F32)
    master_out[0], one_out[0], two_out[0] = adam_update(master_v[...], one_v[...], two_v[...], grad)

    for sent in started:
        sent.copy.wait_send()


STATE = jax.ShapeDtypeStruct((1, ROWS, HID), F32)
RESULTS = (
    STATE,
    STATE,
    STATE,
    jax.ShapeDtypeStruct((1, TBLK, HID), BF16),
)
SLICES = (FRAGS, 1024)


def run_exchange(*operands):
    vmem = pl.BlockSpec(memory_space=pltpu.VMEM)
    return pl.pallas_call(
        exchange,
        name="exchange",
        out_shape=RESULTS + (jax.ShapeDtypeStruct((QUARTERS,) + SLICES, F32),),
        in_specs=[pl.BlockSpec(memory_space=pl.ANY)] * 6,
        out_specs=(vmem,) * 5,
        scratch_shapes=[
            pltpu.VMEM((NX * TBLK, COLS), BF16),
            pltpu.VMEM((COLS, HID), BF16),
            pltpu.VMEM((NX, TBLK, HID), BF16),
            pltpu.VMEM((COLS, HID), F32),
            pltpu.VMEM((3, TBLK, HID), F32),
            pltpu.VMEM((TBLK, HID), BF16),
            pltpu.VMEM((2, TBLK, HID), BF16),
            pltpu.VMEM((2, TBLK // 2, HID), BF16),
            pltpu.VMEM((2, TBLK, HID), BF16),
            pltpu.VMEM((4, ROWS, HID), BF16),
            pltpu.VMEM((4, ROWS, HID), BF16),
            pltpu.VMEM((ROWS, HID), BF16),
            pltpu.VMEM((2, ROWS, HID), BF16),
            pltpu.VMEM((2, ROWS // 2, HID), BF16),
            pltpu.VMEM((2, ROWS, HID), BF16),
            pltpu.VMEM((2,) + SLICES, F32),
            pltpu.VMEM((2,) + SLICES, F32),
            pltpu.VMEM((QUARTERS,) + SLICES, F32),
            pltpu.VMEM((ROWS, HID), F32),
            pltpu.VMEM((ROWS, HID), F32),
            pltpu.VMEM((ROWS, HID), F32),
            pltpu.VMEM((1,) + SLICES, BF16),
            pltpu.SemaphoreType.DMA((N_COPIES,)),
            pltpu.SemaphoreType.DMA((N_COPIES,)),
            pltpu.SemaphoreType.DMA((6,)),
        ],
        compiler_params=pltpu.CompilerParams(
            collective_id=0, has_side_effects=True, vmem_limit_bytes=int(51.85 * 2**20)
        ),
    )(*operands)


def finish(frag_ref, sums, anchor, momentum, master, one, two, up, master_o, one_o, two_o, up_o, anchor_o, momentum_o, buf, sem):
    pairs = ((master, master_o), (one, one_o), (two, two_o), (up, up_o))
    copies = [pltpu.make_async_copy(src, dst, sem.at[i]) for i, (src, dst) in enumerate(pairs)]
    for copy in copies:
        copy.start()
    frag = frag_ref[0]
    for quarter in range(QUARTERS):
        row = slice(quarter, quarter + 1)
        local_sum = sums[quarter, 0:1, :]
        anchor_f = anchor[0, row, :]
        momentum_f = momentum[0, row, :]
        for i in range(1, FRAGS):
            local_sum = jnp.where(frag == i, sums[quarter, i : i + 1, :], local_sum)
            anchor_f = jnp.where(frag == i, anchor[i, row, :], anchor_f)
            momentum_f = jnp.where(frag == i, momentum[i, row, :], momentum_f)
        buf[0, row, :], buf[1, row, :] = nesterov(anchor_f, momentum_f, anchor_f - local_sum * 0.25)
    for i, out in enumerate((anchor_o, momentum_o)):
        copies.append(pltpu.make_async_copy(buf.at[i], out, sem.at[4 + i]))
        copies[-1].start()
    for copy in copies:
        copy.wait()


def run_finish(*given):
    place = pl.BlockSpec(memory_space=pl.ANY)
    vmem = pl.BlockSpec(memory_space=pltpu.VMEM)
    small = jax.ShapeDtypeStruct((QUARTERS, 1024), F32)
    return pl.pallas_call(
        finish,
        name="finish",
        out_shape=RESULTS + (small, small),
        in_specs=[pl.BlockSpec(memory_space=pltpu.SMEM)] + [vmem] * 3 + [place] * 4,
        out_specs=(place,) * 6,
        scratch_shapes=[pltpu.VMEM((2, QUARTERS, 1024), F32), pltpu.SemaphoreType.DMA((6,))],
        compiler_params=pltpu.CompilerParams(vmem_limit_bytes=2**20),
    )(*given)


def local(
    tokens,
    cotangent,
    master,
    moment_one,
    moment_two,
    anchor,
    outer_momentum,
    local_frag,
    frag_index,
):
    *results, sums = run_exchange(tokens, cotangent, master, local_frag, moment_one, moment_two)
    return run_finish(frag_index, sums, anchor, outer_momentum, *results)


def solution(mesh):
    in_specs = (
        P("replica", "fsdp", None),
        P("replica", "fsdp", None),
        P("replica", "fsdp", None),
        P("replica", "fsdp", None),
        P("replica", "fsdp", None),
        P(None, None, "fsdp"),
        P(None, None, "fsdp"),
        P("replica", None, "fsdp"),
        P(),
    )
    out_specs = (
        P("replica", "fsdp", None),
        P("replica", "fsdp", None),
        P("replica", "fsdp", None),
        P("replica", "fsdp", None),
        P(None, "fsdp"),
        P(None, "fsdp"),
    )
    return jax.shard_map(local, mesh=mesh, in_specs=in_specs, out_specs=out_specs, check_vma=False)
```

time: 77.7 us -> 71.4 us (0.919)
  the two profiles are of different devices: /device:TPU:66 before, /device:TPU:1 now
where the time goes in v2:
time: 71.4 us; the launch traced here: 70.9 us
  Pallas kernels  68.8 us (96%)
  between operations  1.32 us (2%)
    pallas_call x1, Pallas kernels, run_exchange(): pl.pallas_call(exchange, name='exchange', out_shape=RESULTS + (jax.ShapeD...  67.6 us

profile of v2, /device:TPU:1, one launch (start us, length us, event | category | flops | bytes accessed | tf_op | source)
XLA Modules:
  0.0 70.9 jit_solution(11331555730101890443)
XLA Ops:
  1.3 0.0 copy-start.2
  1.3 0.7 copy-done.2
  2.0 0.0 copy-start
  2.0 0.0 copy-start.1
  2.0 67.6 %exchange.1 = (f32[1,128,896]{2,1,0:T(8,128)S(1)}, f32[1,128,896]{2,1,0:T(8,128)S(1)}, f32[1,128,896]{2,1,0:T(8,128)S(1)}, bf16[1,256,896]{2,1,0:T(8,128)(2,1)S(1)}, f32[4,4,1024]{2,1,0:T(4,128)S(1)}) custom-call(bf16[1,64,4096]{2,1,0:T(8,128)(2,1)} %tok.1, bf16[1,256,896]{2,1,0:T(8,128)(2,1)} %cot.1, f32[1,128,896]{2,1,0:T(8,128)} %master.1, ...), custom_call_target="tpu_custom_call" | custom-call | tf_op jit(solution)/shard_map/exchange/pallas_call | solution.py:422
  69.6 0.0 copy-done
  69.6 0.0 copy-done.1
  69.6 1.3 %finish.1 = (f32[1,128,896]{2,1,0:T(8,128)}, f32[1,128,896]{2,1,0:T(8,128)}, f32[1,128,896]{2,1,0:T(8,128)}, bf16[1,256,896]{2,1,0:T(8,128)(2,1)}, f32[4,1024]{1,0:T(4,128)}, /*index=5*/f32[4,1024]{1,0:T(4,128)}) custom-call(s32[1]{0:T(128)S(6)} %copy.15.frag_ref, f32[4,4,1024]{2,1,0:T(4,128)S(1)} %get-tuple-element.11.sums, f32[4,4,1024]{2,1,0:T(4,128)S(1)} %copy-done, ...), custom_call_target="tpu_custom_call" | custom-call | tf_op jit(solution)/shard_map/finish/pallas_call | solution.py:488
Async XLA Ops:
  1.3 0.7 copy-start.2
  2.0 67.6 %copy-start = (f32[4,4,1024]{2,1,0:T(4,128)S(1)}, f32[4,4,1024]{2,1,0:T(4,128)}, u32[]{:S(2)}) copy-start(f32[4,4,1024]{2,1,0:T(4,128)} %anchor.1) | copy-start | bytes 196612
  2.0 67.6 %copy-start.1 = (f32[4,4,1024]{2,1,0:T(4,128)S(1)}, f32[4,4,1024]{2,1,0:T(4,128)}, u32[]{:S(2)}) copy-start(f32[4,4,1024]{2,1,0:T(4,128)} %momentum.1) | copy-start | bytes 196612

commit v3 on v2

--- a/solution.py
+++ b/solution.py
@@ -26,10 +26,11 @@
 TOK = 64
 WIDE = 4096
 COLS = WIDE // NX
+HALF = COLS // 2
 HID = 896
 ROWS = 128
 TBLK = QUARTERS * TOK
-N_COPIES = 64
+N_COPIES = 80
 
 
 def adam_decayed(master, moment_one, moment_two):
@@ -52,6 +53,11 @@
 
 def mult(value, by):
     return pl.multiple_of(value, by)
+
+
+ORDER_ONE = ("t0_own t0_xp t0_xm t0_x2 w_pa w_mb w_c0 t1_own c_pa c_mb t0_on3 t0_on1 t0_on2 o1 t1_xp t1_xm t1_x2 t0_re0 c_pb c_ma t0_re3 t0_re1 t0_re2 t1_on3 t1_on1 t1_on2 o2 w_ra w_rb t1_re0 c_ra c_rb t1_re3 w_pb w_ma t1_re1 t1_re2 o3",)
+ORDER_TWO = ("w_c3 w_c1",)
+ORDER_THREE = ("o4 w_c2a w_c2b",)
 
 
 class Sent:
@@ -144,11 +150,14 @@
         started.append(Sent(copy))
         return started[-1]
 
-    def trow(slot, quarter):
-        return tbuf.at[pl.ds(mult(slot * TBLK + quarter * TOK, TOK), TOK), :]
-
-    def piece(dx):
-        return tok.at[0, :, pl.ds(mult(lax.rem(x + dx, 4) * COLS, COLS), COLS)]
+    own_pair = zh // 2
+    pairs = (1 - own_pair, own_pair)
+
+    def trow(rnd, slot, quarter):
+        return tbuf.at[rnd, pl.ds(mult(slot * TBLK + quarter * TOK, TOK), TOK), :]
+
+    def piece(rnd, dx):
+        return tok.at[0, :, pl.ds(mult(lax.rem(x + dx, 4) * COLS + pairs[rnd] * HALF, HALF), HALF)]
 
     def woff(dz, core):
         return lax.rem(zh + dz, 4) * (2 * ROWS) + core * ROWS
@@ -160,7 +169,7 @@
         return wbuf.at[pl.ds(mult(woff(dz, k), ROWS), ROWS), :]
 
     def chalf(slot, half):
-        return cbuf.at[slot, pl.ds(half * (TBLK // 2), TBLK // 2), :]
+        return cbuf.at[pl.ds(slot * TBLK + half * (TBLK // 2), TBLK // 2), :]
 
     def own_chalf(half):
         return cot.at[0, pl.ds(half * (TBLK // 2), TBLK // 2), :]
@@ -170,9 +179,10 @@
         for i, (src, dst) in enumerate(
             (
                 (master.at[0], master_v),
-                (piece(0), trow(0, c)),
+                (piece(0, 0), trow(0, 0, c)),
+                (piece(1, 0), trow(1, 0, c)),
                 (local_hbm, local_frag),
-                (cot.at[0], cbuf.at[0]),
+                (cot.at[0], cbuf.at[pl.ds(0, TBLK), :]),
                 (one_hbm.at[0], one_v),
                 (two_hbm.at[0], two_v),
             )
@@ -180,7 +190,7 @@
     ]
     for load in loads:
         load.start()
-    l_master, l_tok, l_local, l_cot, l_one, l_two = loads
+    l_master, l_tok, l_tok2, l_local, l_cot, l_one, l_two = loads
 
     l_master.wait()
     wbuf[pl.ds(mult(woff(0, k), ROWS), ROWS), :] = master_v[...].astype(BF16)
@@ -192,7 +202,7 @@
     cp = {}
 
     def own_outer():
-        for load in (l_tok, l_local, l_cot, l_one, l_two):
+        for load in (l_tok, l_tok2, l_local, l_cot, l_one, l_two):
             load.wait()
         o_part[0] = local_frag[0].astype(F32)
         cp["o1"] = send(o_part.at[0], o_in.at[0], y2)
@@ -226,36 +236,28 @@
 
         return step
 
-    def t_on(slot):
+    def t_on(rnd, slot):
         def step():
-            t_l[slot] = send(trow(slot, c), trow(slot, c), pl_)
-            t_y[slot] = send(trow(slot, c), trow(slot, c), py)
+            t_l[rnd, slot] = send(trow(rnd, slot, c), trow(rnd, slot, c), pl_)
+            t_y[rnd, slot] = send(trow(rnd, slot, c), trow(rnd, slot, c), py)
 
         return step
 
-    def t_relay(slot):
+    def t_relay(rnd, slot):
         def step():
-            t_l[slot].wait_recv()
-            t_r[slot] = send(trow(slot, c_l), trow(slot, c_l), py)
+            t_l[rnd, slot].wait_recv()
+            t_r[rnd, slot] = send(trow(rnd, slot, c_l), trow(rnd, slot, c_l), py)
 
         return step
 
-    def t_own():
-        t_y[0] = send(piece(0), trow(0, c), py)
-        t_l[0] = send(piece(0), trow(0, c), pl_)
+    def t_own(rnd):
+        def step():
+            t_y[rnd, 0] = send(piece(rnd, 0), trow(rnd, 0, c), py)
+            t_l[rnd, 0] = send(piece(rnd, 0), trow(rnd, 0, c), pl_)
+
+        return step
 
     steps = {
-        "t_own": t_own,
-        "t_xp": put("t_xp", piece(1), trow(3, c), xp),
-        "t_xm": put("t_xm", piece(3), trow(1, c), xm),
-        "t_x2": put("t_x2", piece(2), trow(2, c), x2),
-        "t_on3": after("t_xp", t_on(3)),
-        "t_on1": after("t_xm", t_on(1)),
-        "t_on2": after("t_x2", t_on(2)),
-        "t_re0": t_relay(0),
-        "t_re1": t_relay(1),
-        "t_re2": t_relay(2),
-        "t_re3": t_relay(3),
         "w_pa": put("w_pa", whalf(0, 0), whalf(0, 0), zp),
         "w_mb": put("w_mb", whalf(0, 1), whalf(0, 1), zm),
         "w_pb": put("w_pb", whalf(0, 1), whalf(0, 1), zp),
@@ -278,55 +280,78 @@
         "o3": outer_three,
         "o4": outer_four,
     }
-    order = (
-        "t_own t_xp t_xm t_x2 w_pa w_mb w_c0 o1 t_on3 t_on1 c_pa c_mb t_re0 t_on2 c_pb c_ma w_pb w_ma o2 "
-        "w_ra w_rb t_re3 c_ra c_rb t_re1 t_re2 o3 w_c3 w_c1 o4"
-    )
-    for step in order.split():
-        steps[step]()
-
-    def add_grad(slot, first=False):
-        part = cbuf.at[slot]
-
-        def tile(j, carry):
-            cols = pl.ds(mult(j * 256, 256), 256)
-            left = tbuf[slot * TBLK : (slot + 1) * TBLK, cols]
-            prod = lax.dot_general(left, part[...], (((0,), (0,)), ((), ())), preferred_element_type=F32)
-            if first:
-                acc[cols, :] = prod
-            else:
-                acc[cols, :] += prod
-            return carry
-
-        lax.fori_loop(0, COLS // 256, tile, 0)
+    for r in range(2):
+        steps[f"t{r}_own"] = t_own(r)
+        for slot, name, to in ((3, "xp", xp), (1, "xm", xm), (2, "x2", x2)):
+            steps[f"t{r}_{name}"] = put(f"t{r}_{name}", piece(r, 4 - slot), trow(r, slot, c), to)
+            steps[f"t{r}_on{slot}"] = after(f"t{r}_{name}", t_on(r, slot))
+        for slot in range(NX):
+            steps[f"t{r}_re{slot}"] = t_relay(r, slot)
+
+    def run(order):
+        for step in " ".join(order).split():
+            steps[step]()
+
+    run(ORDER_ONE)
+
+    half_t = TBLK // 2
+    half_r = ROWS // 2
+    odd = lax.rem(zh, 2)
+    far = lax.rem(zh + 2, 4)
+    blocks = (far, 3 - zh, zh + 1 - 2 * odd, zh)
+    core_copies = []
+
+    def tokens_here(rnd, slot):
+        t_y[rnd, slot].wait_recv()
+        t_r[rnd, slot].wait_recv()
+
+    def grad_part(i, lo, hi):
+        rnd = i // 2
+        col = pl.ds(mult(lax.rem(blocks[i], 2) * 256, 256), 256)
+        left = tbuf[rnd, lo * TBLK : hi * TBLK, col]
+        right = cbuf[lo * TBLK : hi * TBLK, :]
+        return lax.dot_general(left, right, (((0,), (0,)), ((), ())), preferred_element_type=F32)
+
+    def both_rows(i):
+        return pl.ds(mult(blocks[i] * 2 * ROWS, 2 * ROWS), 2 * ROWS)
+
+    def rows_of(i, core):
+        return pl.ds(mult(blocks[i] * 2 * ROWS + core * ROWS, ROWS), ROWS)
+
+    def core_send(i):
+        g_core[i] = acc[rows_of(i, 1 - k), :].astype(BF16)
+        core_copies.append(send(g_core.at[i], g_core_in.at[i], co))
+
+    def core_sum(i):
+        core_copies[i].wait_recv()
+        total = acc[rows_of(i, k), :] + g_core_in[i].astype(F32)
+        acc[rows_of(i, k), :] = total
+        return total
 
     def up_part(slot, store):
-        left = slice(slot * TBLK, (slot + 1) * TBLK)
+        rows = slice(slot * TBLK, (slot + 1) * TBLK)
         for lo in range(0, HID, 256):
             hi = min(lo + 256, HID)
-            store(lo, hi, jnp.dot(tbuf[left, :], wbuf[:, lo:hi], preferred_element_type=F32))
-
-    def tokens_here(slot):
-        t_y[slot].wait_recv()
-        t_r[slot].wait_recv()
-
-    half_t = TBLK // 2
-    half_r = ROWS // 2
-    tokens_here(0)
-    add_grad(0, True)
-
-    steps["w_c2a"]()
-    steps["w_c2b"]()
-    cp["o4"].wait_recv()
-    sum_out[...] = o_all[...]
-    master_v[...], one_v[...], two_v[...] = adam_decayed(master_v[...], one_v[...], two_v[...])
+            total = None
+            for rnd in range(2):
+                weights = wbuf[pl.ds(mult(pairs[rnd] * HALF, HALF), HALF), lo:hi]
+                part = jnp.dot(tbuf[rnd, rows, :], weights, preferred_element_type=F32)
+                total = part if total is None else total + part
+            store(lo, hi, total)
 
     for name in ("c_ra", "c_rb", "c_pb", "c_ma"):
         cp[name].wait_recv()
-    tokens_here(2)
-    add_grad(2)
-    for name in ("w_c0", "w_c1", "w_c3", "w_c2a", "w_c2b"):
-        cp[name].wait_recv()
+    for slot in range(NX):
+        tokens_here(0, slot)
+    for i in (0, 1):
+        acc[both_rows(i), :] = grad_part(i, 0, NX)
+        core_send(i)
+    run(ORDER_TWO)
+    g_far[...] = core_sum(0).astype(BF16)
+    g_fp = send(g_far.at[pl.ds(0, half_r), :], g_in.at[0], zp)
+    g_fm = send(g_far.at[pl.ds(half_r, half_r), :], g_in.at[1], zm)
+    core_sum(1)
+    run(ORDER_THREE)
 
     def store_far(lo, hi, value):
         up_far[:, lo:hi] = value.astype(BF16)
@@ -337,44 +362,44 @@
 
         return store
 
+    master_v[...], one_v[...], two_v[...] = adam_decayed(master_v[...], one_v[...], two_v[...])
+    for name in ("w_c0", "w_c1", "w_c3", "w_c2a", "w_c2b"):
+        cp[name].wait_recv()
+    tokens_here(1, 2)
     up_part(2, store_far)
     u_fp = send(up_far.at[pl.ds(0, half_t), :], up_in.at[0], xp)
     u_fm = send(up_far.at[pl.ds(half_t, half_t), :], up_in.at[1], xm)
 
-    tokens_here(3)
-    add_grad(3)
+    tokens_here(1, 0)
+    tokens_here(1, 1)
+    tokens_here(1, 3)
+    for i in (2, 3):
+        acc[both_rows(i), :] = grad_part(i, 0, NX)
+        core_send(i)
+
     up_part(3, store_f(2))
     up_near[1, :half_t, :] = upf[2, :half_t, :].astype(BF16)
     u_ma = send(up_near.at[1, pl.ds(0, half_t), :], up_got.at[1, pl.ds(0, half_t), :], xm)
 
-    tokens_here(1)
-    core_copies = {}
-    for e in (2, 1, 3, 0):
-        both = pl.ds(mult(woff(e, 0), 2 * ROWS), 2 * ROWS)
-        left = tbuf[TBLK : 2 * TBLK, both]
-        acc[both, :] += lax.dot_general(left, cbuf[1], (((0,), (0,)), ((), ())), preferred_element_type=F32)
-        g_core[e] = acc[pl.ds(mult(woff(e, 1 - k), ROWS), ROWS), :].astype(BF16)
-        core_copies[e] = send(g_core.at[e], g_core_in.at[e], co)
-
-    def core_sum(e):
-        rows = pl.ds(mult(woff(e, k), ROWS), ROWS)
-        core_copies[e].wait_recv()
-        total = acc[rows, :] + g_core_in[e].astype(F32)
-        acc[rows, :] = total
-        return total
-
-    g_far[...] = core_sum(2).astype(BF16)
-    g_fp = send(g_far.at[pl.ds(0, half_r), :], g_in.at[0], zp)
-    g_fm = send(g_far.at[pl.ds(half_r, half_r), :], g_in.at[1], zm)
-    g_near[0] = core_sum(1).astype(BF16)
+    core_sum(2)
+    near = [pl.ds(mult(woff(e, k), ROWS), ROWS) for e in (1, 3)]
+    g_near[0] = acc[near[0], :].astype(BF16)
     g_pb = send(g_near.at[0, pl.ds(half_r, half_r), :], g_got.at[0, pl.ds(half_r, half_r), :], zp)
-    g_near[1] = core_sum(3).astype(BF16)
+    g_near[1] = acc[near[1], :].astype(BF16)
     g_ma = send(g_near.at[1, pl.ds(0, half_r), :], g_got.at[1, pl.ds(0, half_r), :], zm)
-    core_sum(0)
 
     up_part(1, store_f(1))
     up_near[0, half_t:, :] = upf[1, half_t:, :].astype(BF16)
     u_pb = send(up_near.at[0, pl.ds(half_t, half_t), :], up_got.at[0, pl.ds(half_t, half_t), :], xp)
+    def row_half(dz, half):
+        return pl.ds(mult(woff(dz, k) + half * half_r, half_r), half_r)
+
+    g_fp.wait_recv()
+    g_near[0, :half_r, :] = (acc[row_half(1, 0), :] + g_in[0].astype(F32)).astype(BF16)
+    g_pa = send(g_near.at[0, pl.ds(0, half_r), :], g_got.at[0, pl.ds(0, half_r), :], zp)
+    g_fm.wait_recv()
+    g_near[1, half_r:, :] = (acc[row_half(3, 1), :] + g_in[1].astype(F32)).astype(BF16)
+    g_mb = send(g_near.at[1, pl.ds(half_r, half_r), :], g_got.at[1, pl.ds(half_r, half_r), :], zm)
 
     u_fm.wait_recv()
     up_near[1, half_t:, :] = (upf[2, half_t:, :] + up_in[1].astype(F32)).astype(BF16)
@@ -383,16 +408,9 @@
     up_near[0, :half_t, :] = (upf[1, :half_t, :] + up_in[0].astype(F32)).astype(BF16)
     u_pa = send(up_near.at[0, pl.ds(0, half_t), :], up_got.at[0, pl.ds(0, half_t), :], xp)
     up_part(0, store_f(0))
-
-    def row_half(dz, half):
-        return pl.ds(mult(woff(dz, k) + half * half_r, half_r), half_r)
-
-    g_fp.wait_recv()
-    g_near[0, :half_r, :] = (acc[row_half(1, 0), :] + g_in[0].astype(F32)).astype(BF16)
-    g_pa = send(g_near.at[0, pl.ds(0, half_r), :], g_got.at[0, pl.ds(0, half_r), :], zp)
-    g_fm.wait_recv()
-    g_near[1, half_r:, :] = (acc[row_half(3, 1), :] + g_in[1].astype(F32)).astype(BF16)
-    g_mb = send(g_near.at[1, pl.ds(half_r, half_r), :], g_got.at[1, pl.ds(half_r, half_r), :], zm)
+    core_sum(3)
+    cp["o4"].wait_recv()
+    sum_out[...] = o_all[...]
 
     for copy in (u_pb, u_ma, u_pa, u_mb):
         copy.wait_recv()
@@ -426,9 +444,9 @@
         in_specs=[pl.BlockSpec(memory_space=pl.ANY)] * 6,
         out_specs=(vmem,) * 5,
         scratch_shapes=[
-            pltpu.VMEM((NX * TBLK, COLS), BF16),
+            pltpu.VMEM((2, NX * TBLK, HALF), BF16),
             pltpu.VMEM((COLS, HID), BF16),
-            pltpu.VMEM((NX, TBLK, HID), BF16),
+            pltpu.VMEM((NX * TBLK, HID), BF16),
             pltpu.VMEM((COLS, HID), F32),
             pltpu.VMEM((3, TBLK, HID), F32),
             pltpu.VMEM((TBLK, HID), BF16),
@@ -450,7 +468,7 @@
             pltpu.VMEM((1,) + SLICES, BF16),
             pltpu.SemaphoreType.DMA((N_COPIES,)),
             pltpu.SemaphoreType.DMA((N_COPIES,)),
-            pltpu.SemaphoreType.DMA((6,)),
+            pltpu.SemaphoreType.DMA((7,)),
         ],
         compiler_params=pltpu.CompilerParams(
             collective_id=0, has_side_effects=True, vmem_limit_bytes=int(51.85 * 2**20)

time: 71.4 us -> 68.6 us (0.961)
  Pallas kernels: 68.8 us -> 66.4 us
    pallas_call x1, Pallas kernels: 67.6 us -> 65.1 us  [run_exchange(): pl.pallas_call(exchange, name='exchange', out_shape=RESULTS + (jax.ShapeD...]
where the time goes in v3:
time: 68.6 us; the launch traced here: 68.4 us
  Pallas kernels  66.4 us (97%)
  between operations  1.32 us (2%)
  local copies, waits for them, and re-layouts  0.7 us (1%)
    pallas_call x1, Pallas kernels, run_exchange(): pl.pallas_call(exchange, name='exchange', out_shape=RESULTS + (jax.ShapeD...  65.1 us

profile of v3, /device:TPU:1, one launch (start us, length us, event | category | flops | bytes accessed | tf_op | source)
XLA Modules:
  0.0 68.4 jit_solution(15390747152504650111)
XLA Ops:
  1.3 0.0 copy-start.2
  1.3 0.7 %copy-done.2 = bf16[1,4,1024]{2,1,0:T(4,128)(2,1)S(1)} copy-done((bf16[1,4,1024]{2,1,0:T(4,128)(2,1)S(1)}, bf16[1,4,1024]{2,1,0:T(4,128)(2,1)}, u32[]{:S(2)}) %copy-start.2) | copy-done | bytes 8216
  2.0 0.0 copy-start
  2.0 0.0 copy-start.1
  2.0 65.1 %exchange.1 = (f32[1,128,896]{2,1,0:T(8,128)S(1)}, f32[1,128,896]{2,1,0:T(8,128)S(1)}, f32[1,128,896]{2,1,0:T(8,128)S(1)}, bf16[1,256,896]{2,1,0:T(8,128)(2,1)S(1)}, f32[4,4,1024]{2,1,0:T(4,128)S(1)}) custom-call(bf16[1,64,4096]{2,1,0:T(8,128)(2,1)} %tok.1, bf16[1,256,896]{2,1,0:T(8,128)(2,1)} %cot.1, f32[1,128,896]{2,1,0:T(8,128)} %master.1, ...), custom_call_target="tpu_custom_call" | custom-call | tf_op jit(solution)/shard_map/exchange/pallas_call | solution.py:440
  67.1 0.0 copy-done
  67.1 0.0 copy-done.1
  67.1 1.3 %finish.1 = (f32[1,128,896]{2,1,0:T(8,128)}, f32[1,128,896]{2,1,0:T(8,128)}, f32[1,128,896]{2,1,0:T(8,128)}, bf16[1,256,896]{2,1,0:T(8,128)(2,1)}, f32[4,1024]{1,0:T(4,128)}, /*index=5*/f32[4,1024]{1,0:T(4,128)}) custom-call(s32[1]{0:T(128)S(6)} %copy.15.frag_ref, f32[4,4,1024]{2,1,0:T(4,128)S(1)} %get-tuple-element.11.sums, f32[4,4,1024]{2,1,0:T(4,128)S(1)} %copy-done, ...), custom_call_target="tpu_custom_call" | custom-call | tf_op jit(solution)/shard_map/finish/pallas_call | solution.py:506
Async XLA Ops:
  1.3 0.7 %copy-start.2 = (bf16[1,4,1024]{2,1,0:T(4,128)(2,1)S(1)}, bf16[1,4,1024]{2,1,0:T(4,128)(2,1)}, u32[]{:S(2)}) copy-start(bf16[1,4,1024]{2,1,0:T(4,128)(2,1)} %local_hbm.1) | copy-start | bytes 24580
  2.0 65.1 %copy-start = (f32[4,4,1024]{2,1,0:T(4,128)S(1)}, f32[4,4,1024]{2,1,0:T(4,128)}, u32[]{:S(2)}) copy-start(f32[4,4,1024]{2,1,0:T(4,128)} %anchor.1) | copy-start | bytes 196612
  2.0 65.1 %copy-start.1 = (f32[4,4,1024]{2,1,0:T(4,128)S(1)}, f32[4,4,1024]{2,1,0:T(4,128)}, u32[]{:S(2)}) copy-start(f32[4,4,1024]{2,1,0:T(4,128)} %momentum.1) | copy-start | bytes 196612

commit v4 on v3

--- a/solution.py
+++ b/solution.py
@@ -55,9 +55,9 @@
     return pl.multiple_of(value, by)
 
 
-ORDER_ONE = ("t0_own t0_xp t0_xm t0_x2 w_pa w_mb w_c0 t1_own c_pa c_mb t0_on3 t0_on1 t0_on2 o1 t1_xp t1_xm t1_x2 t0_re0 c_pb c_ma t0_re3 t0_re1 t0_re2 t1_on3 t1_on1 t1_on2 o2 w_ra w_rb t1_re0 c_ra c_rb t1_re3 w_pb w_ma t1_re1 t1_re2 o3",)
+ORDER_ONE = ("t0_own t0_xp t0_xm t0_x2 w_own w_pa w_mb w_c0 t1_own c_pa c_mb t0_on3 t0_on1 t0_on2 o1 t1_xp t1_xm t1_x2 t0_re0 c_pb c_ma t0_re3 t0_re1 t0_re2 t1_on3 t1_on1 t1_on2 o2 w_ra w_rb t1_re0 c_ra c_rb t1_re3 w_pb w_ma t1_re1 t1_re2 o3",)
 ORDER_TWO = ("w_c3 w_c1",)
-ORDER_THREE = ("o4 w_c2a w_c2b",)
+ORDER_THREE = ("w_c2a w_c2b",)
 
 
 class Sent:
@@ -192,9 +192,6 @@
         load.start()
     l_master, l_tok, l_tok2, l_local, l_cot, l_one, l_two = loads
 
-    l_master.wait()
-    wbuf[pl.ds(mult(woff(0, k), ROWS), ROWS), :] = master_v[...].astype(BF16)
-
     pl.semaphore_wait(barrier, len(partners))
 
     t_y, t_l, t_r = {}, {}, {}
@@ -257,7 +254,12 @@
 
         return step
 
+    def own_rows():
+        l_master.wait()
+        wbuf[pl.ds(mult(woff(0, k), ROWS), ROWS), :] = master_v[...].astype(BF16)
+
     steps = {
+        "w_own": own_rows,
         "w_pa": put("w_pa", whalf(0, 0), whalf(0, 0), zp),
         "w_mb": put("w_mb", whalf(0, 1), whalf(0, 1), zm),
         "w_pb": put("w_pb", whalf(0, 1), whalf(0, 1), zp),
@@ -388,6 +390,7 @@
     g_near[1] = acc[near[1], :].astype(BF16)
     g_ma = send(g_near.at[1, pl.ds(0, half_r), :], g_got.at[1, pl.ds(0, half_r), :], zm)
 
+    steps["o4"]()
     up_part(1, store_f(1))
     up_near[0, half_t:, :] = upf[1, half_t:, :].astype(BF16)
     u_pb = send(up_near.at[0, pl.ds(half_t, half_t), :], up_got.at[0, pl.ds(half_t, half_t), :], xp)
@@ -412,14 +415,15 @@
     cp["o4"].wait_recv()
     sum_out[...] = o_all[...]
 
-    for copy in (u_pb, u_ma, u_pa, u_mb):
-        copy.wait_recv()
-    up_out[0] = (upf[0] + up_got[0].astype(F32) + up_got[1].astype(F32)).astype(BF16)
     for copy in (g_pb, g_ma, g_pa, g_mb):
         copy.wait_recv()
     own = pl.ds(mult(woff(0, k), ROWS), ROWS)
     grad = acc[own, :] + g_got[0].astype(F32) + g_got[1].astype(F32)
     master_out[0], one_out[0], two_out[0] = adam_update(master_v[...], one_v[...], two_v[...], grad)
+
+    for copy in (u_pb, u_ma, u_pa, u_mb):
+        copy.wait_recv()
+    up_out[0] = (upf[0] + up_got[0].astype(F32) + up_got[1].astype(F32)).astype(BF16)
 
     for sent in started:
         sent.copy.wait_send()

time: 68.6 us -> 68.3 us (level)
  no operation moved by 1% of the time
where the time goes in v4:
time: 68.3 us; the launch traced here: 68.1 us
  Pallas kernels  66.1 us (97%)
  between operations  1.32 us (2%)
  local copies, waits for them, and re-layouts  0.7 us (1%)
    pallas_call x1, Pallas kernels, run_exchange(): pl.pallas_call(exchange, name='exchange', out_shape=RESULTS + (jax.ShapeD...  64.8 us

profile of v4, /device:TPU:1, one launch (start us, length us, event | category | flops | bytes accessed | tf_op | source)
XLA Modules:
  0.0 68.1 jit_solution(1730091931201137202)
XLA Ops:
  1.3 0.0 copy-start.2
  1.3 0.7 %copy-done.2 = bf16[1,4,1024]{2,1,0:T(4,128)(2,1)S(1)} copy-done((bf16[1,4,1024]{2,1,0:T(4,128)(2,1)S(1)}, bf16[1,4,1024]{2,1,0:T(4,128)(2,1)}, u32[]{:S(2)}) %copy-start.2) | copy-done | bytes 8216
  2.0 0.0 copy-start
  2.0 0.0 copy-start.1
  2.0 64.8 %exchange.1 = (f32[1,128,896]{2,1,0:T(8,128)S(1)}, f32[1,128,896]{2,1,0:T(8,128)S(1)}, f32[1,128,896]{2,1,0:T(8,128)S(1)}, bf16[1,256,896]{2,1,0:T(8,128)(2,1)S(1)}, f32[4,4,1024]{2,1,0:T(4,128)S(1)}) custom-call(bf16[1,64,4096]{2,1,0:T(8,128)(2,1)} %tok.1, bf16[1,256,896]{2,1,0:T(8,128)(2,1)} %cot.1, f32[1,128,896]{2,1,0:T(8,128)} %master.1, ...), custom_call_target="tpu_custom_call" | custom-call | tf_op jit(solution)/shard_map/exchange/pallas_call | solution.py:444
  66.8 0.0 copy-done
  66.8 0.0 copy-done.1
  66.8 1.3 %finish.1 = (f32[1,128,896]{2,1,0:T(8,128)}, f32[1,128,896]{2,1,0:T(8,128)}, f32[1,128,896]{2,1,0:T(8,128)}, bf16[1,256,896]{2,1,0:T(8,128)(2,1)}, f32[4,1024]{1,0:T(4,128)}, /*index=5*/f32[4,1024]{1,0:T(4,128)}) custom-call(s32[1]{0:T(128)S(6)} %copy.15.frag_ref, f32[4,4,1024]{2,1,0:T(4,128)S(1)} %get-tuple-element.11.sums, f32[4,4,1024]{2,1,0:T(4,128)S(1)} %copy-done, ...), custom_call_target="tpu_custom_call" | custom-call | tf_op jit(solution)/shard_map/finish/pallas_call | solution.py:510
Async XLA Ops:
  1.3 0.7 %copy-start.2 = (bf16[1,4,1024]{2,1,0:T(4,128)(2,1)S(1)}, bf16[1,4,1024]{2,1,0:T(4,128)(2,1)}, u32[]{:S(2)}) copy-start(bf16[1,4,1024]{2,1,0:T(4,128)(2,1)} %local_hbm.1) | copy-start | bytes 24580
  2.0 64.8 %copy-start = (f32[4,4,1024]{2,1,0:T(4,128)S(1)}, f32[4,4,1024]{2,1,0:T(4,128)}, u32[]{:S(2)}) copy-start(f32[4,4,1024]{2,1,0:T(4,128)} %anchor.1) | copy-start | bytes 196612
  2.0 64.8 %copy-start.1 = (f32[4,4,1024]{2,1,0:T(4,128)S(1)}, f32[4,4,1024]{2,1,0:T(4,128)}, u32[]{:S(2)}) copy-start(f32[4,4,1024]{2,1,0:T(4,128)} %momentum.1) | copy-start | bytes 196612

commit v5 on v4

--- a/solution.py
+++ b/solution.py
@@ -55,9 +55,14 @@
     return pl.multiple_of(value, by)
 
 
-ORDER_ONE = ("t0_own t0_xp t0_xm t0_x2 w_own w_pa w_mb w_c0 t1_own c_pa c_mb t0_on3 t0_on1 t0_on2 o1 t1_xp t1_xm t1_x2 t0_re0 c_pb c_ma t0_re3 t0_re1 t0_re2 t1_on3 t1_on1 t1_on2 o2 w_ra w_rb t1_re0 c_ra c_rb t1_re3 w_pb w_ma t1_re1 t1_re2 o3",)
-ORDER_TWO = ("w_c3 w_c1",)
-ORDER_THREE = ("w_c2a w_c2b",)
+ORDER_ONE = (
+    "t0_own", "t0_xp", "t0_xm", "t0_x2", "w_own", "w_pa", "w_mb", "w_c0", "t1_own", "c_pa", "c_mb", "t0_on3",
+    "t0_on1", "t0_on2", "o1", "t1_xp", "t1_xm", "t1_x2", "t0_re0", "c_pb", "c_ma", "t0_re3", "t0_re1", "t0_re2",
+    "t1_on3", "t1_on1", "t1_on2", "o2", "w_ra", "w_rb", "t1_re0", "c_ra", "c_rb", "t1_re3", "w_pb", "w_ma", "t1_re1",
+    "t1_re2", "o3",
+)
+ORDER_TWO = ("w_c3", "w_c1")
+ORDER_THREE = ("w_c2a", "w_c2b")
 
 
 class Sent:
@@ -291,7 +296,7 @@
             steps[f"t{r}_re{slot}"] = t_relay(r, slot)
 
     def run(order):
-        for step in " ".join(order).split():
+        for step in order:
             steps[step]()
 
     run(ORDER_ONE)

time: 68.3 us -> 68.3 us (level)
  no operation moved by 1% of the time
where the time goes in v5:
time: 68.3 us; the launch traced here: 68.1 us
  Pallas kernels  66.1 us (97%)
  between operations  1.32 us (2%)
  local copies, waits for them, and re-layouts  0.7 us (1%)
    pallas_call x1, Pallas kernels, run_exchange(): pl.pallas_call(exchange, name='exchange', out_shape=RESULTS + (jax.ShapeD...  64.8 us

profile of v5, /device:TPU:1, one launch (start us, length us, event | category | flops | bytes accessed | tf_op | source)
XLA Modules:
  0.0 68.1 jit_solution(1730091931201137202)
XLA Ops:
  1.3 0.0 copy-start.2
  1.3 0.7 %copy-done.2 = bf16[1,4,1024]{2,1,0:T(4,128)(2,1)S(1)} copy-done((bf16[1,4,1024]{2,1,0:T(4,128)(2,1)S(1)}, bf16[1,4,1024]{2,1,0:T(4,128)(2,1)}, u32[]{:S(2)}) %copy-start.2) | copy-done | bytes 8216
  2.0 0.0 copy-start
  2.0 0.0 copy-start.1
  2.0 64.8 %exchange.1 = (f32[1,128,896]{2,1,0:T(8,128)S(1)}, f32[1,128,896]{2,1,0:T(8,128)S(1)}, f32[1,128,896]{2,1,0:T(8,128)S(1)}, bf16[1,256,896]{2,1,0:T(8,128)(2,1)S(1)}, f32[4,4,1024]{2,1,0:T(4,128)S(1)}) custom-call(bf16[1,64,4096]{2,1,0:T(8,128)(2,1)} %tok.1, bf16[1,256,896]{2,1,0:T(8,128)(2,1)} %cot.1, f32[1,128,896]{2,1,0:T(8,128)} %master.1, ...), custom_call_target="tpu_custom_call" | custom-call | tf_op jit(solution)/shard_map/exchange/pallas_call | solution.py:449
  66.8 0.0 copy-done
  66.8 0.0 copy-done.1
  66.8 1.3 %finish.1 = (f32[1,128,896]{2,1,0:T(8,128)}, f32[1,128,896]{2,1,0:T(8,128)}, f32[1,128,896]{2,1,0:T(8,128)}, bf16[1,256,896]{2,1,0:T(8,128)(2,1)}, f32[4,1024]{1,0:T(4,128)}, /*index=5*/f32[4,1024]{1,0:T(4,128)}) custom-call(s32[1]{0:T(128)S(6)} %copy.15.frag_ref, f32[4,4,1024]{2,1,0:T(4,128)S(1)} %get-tuple-element.11.sums, f32[4,4,1024]{2,1,0:T(4,128)S(1)} %copy-done, ...), custom_call_target="tpu_custom_call" | custom-call | tf_op jit(solution)/shard_map/finish/pallas_call | solution.py:515
Async XLA Ops:
  1.3 0.7 %copy-start.2 = (bf16[1,4,1024]{2,1,0:T(4,128)(2,1)S(1)}, bf16[1,4,1024]{2,1,0:T(4,128)(2,1)}, u32[]{:S(2)}) copy-start(bf16[1,4,1024]{2,1,0:T(4,128)(2,1)} %local_hbm.1) | copy-start | bytes 24580
  2.0 64.8 %copy-start = (f32[4,4,1024]{2,1,0:T(4,128)S(1)}, f32[4,4,1024]{2,1,0:T(4,128)}, u32[]{:S(2)}) copy-start(f32[4,4,1024]{2,1,0:T(4,128)} %anchor.1) | copy-start | bytes 196612
  2.0 64.8 %copy-start.1 = (f32[4,4,1024]{2,1,0:T(4,128)S(1)}, f32[4,4,1024]{2,1,0:T(4,128)}, u32[]{:S(2)}) copy-start(f32[4,4,1024]{2,1,0:T(4,128)} %momentum.1) | copy-start | bytes 196612
